TPU v7x, 32 devices: a whole 2x2x4 slice. The times are simulated.
32 devices in a mesh: grp: 4 (over x, core), gx: 2 (over y), gy: 4 (over z).
Axes of the slice: x: 2, y: 2, z: 4, core: 2. Of those that a mesh axis runs over, the one named last changes fastest.
Arguments:
- slot_field: float32 [4, 2, 96, 512], P('grp', None, 'gx', 'gy'), may hold values from -6 to 6
- solid: int32 [2, 96, 512], P(None, 'gx', 'gy'), may hold values 0 or 1
- lift_weight: bfloat16 [3, 64], replicated, may hold values from -3.5 to 3.5
- spectral_weight: bfloat16 [2048, 128], replicated, may hold values from -1.5 to 1.5
- mix_weight: bfloat16 [64, 64], replicated, may hold values from -0.75 to 0.75
- project_weight: bfloat16 [64, 3], replicated, may hold values from -0.75 to 0.75
- mode_index: int32 [32], replicated, may hold values from 0 to 47, as said below
Outputs:
- new_velocity: float32 [3, 2, 96, 512], P(None, None, 'gx', 'gy')
- spectral_grad: float32 [2048, 128], P(('grp', 'gx', 'gy'))
- mix_grad: float32 [64, 64], replicated
Inputs may be any that keep to these rules, and one draw needn't show every extreme that they name: `mode_index`: 32 distinct values in ascending order; 0 and 47 are always among them.
All inputs are finite; a program needn't handle non-finite values. No bound on the sum of `solid` on one device may be relied on, other than what follows from the above.
Results may differ from a plain program's by a relative error of at most 0.0013.
Values may be sent and summed in bfloat16 or wider, within the bound.
A program may use at most 64 MiB of HBM per device.

v0:
```python
import math

import jax
import jax.numpy as jnp
from jax import lax
from jax.sharding import PartitionSpec as P

VISCOSITY = 0.05
TIME_STEP = 0.1


def with_halo(block, sides, width):
    for axis, dim in sides:
        count = lax.axis_size(axis)
        forward = [(i, i + 1) for i in range(count - 1)]
        backward = [(target, source) for source, target in forward]
        low = lax.ppermute(
            lax.slice_in_dim(block, block.shape[dim] - width, None, axis=dim), axis, forward
        )
        high = lax.ppermute(lax.slice_in_dim(block, 0, width, axis=dim), axis, backward)
        block = jnp.concatenate([low, block, high], axis=dim)
    return block


def interior(source):
    return source[1:-1, 1:-1, 1:-1]


def along_x(source):
    return 0.5 * (source[1:-1, 2:, 1:-1] - source[1:-1, :-2, 1:-1])


def along_y(source):
    return 0.5 * (source[1:-1, 1:-1, 2:] - source[1:-1, 1:-1, :-2])


def along_z(source):
    return 0.5 * (source[2:, 1:-1, 1:-1] - source[:-2, 1:-1, 1:-1])


def laplace(source):
    total = source[2:, 1:-1, 1:-1] + source[:-2, 1:-1, 1:-1]
    total = total + source[1:-1, 2:, 1:-1] + source[1:-1, :-2, 1:-1]
    total = total + source[1:-1, 1:-1, 2:] + source[1:-1, 1:-1, :-2]
    return total - 6.0 * interior(source)


def section_component(padded, component, solid):
    source = padded[component]
    velocity = [interior(padded[index]) for index in range(3)]
    advect = (
        velocity[0] * along_x(source)
        + velocity[1] * along_y(source)
        + velocity[2] * along_z(source)
    )
    pressure = padded[3]
    press_grad = jnp.stack([along_x(pressure), along_y(pressure), along_z(pressure)])[component]
    update = interior(source) + TIME_STEP * (VISCOSITY * laplace(source) - advect - press_grad)
    return update * (1.0 - solid.astype(jnp.float32))


def spectral_table(mode_index, x_length):
    places = jnp.arange(x_length, dtype=jnp.int32)
    phases = mode_index[:, None] * places[None, :] % x_length
    angles = 2.0 * jnp.pi / x_length * phases.astype(jnp.float32)
    return jnp.concatenate([jnp.cos(angles), -jnp.sin(angles)], axis=0).astype(jnp.bfloat16)


def contract(form, left, right):
    return jnp.einsum(form, left, right, preferred_element_type=jnp.float32)


def student_terms(
    line_data,
    dft_table,
    lift_weight,
    spectral_weight,
    mix_weight,
    project_weight,
    loss_scale,
    x_length,
):
    mode_count = dft_table.shape[0] // 2
    chan_count = mix_weight.shape[0]
    scale_dft = 1.0 / math.sqrt(x_length)
    old_part = line_data[:3]
    target = line_data[3:].astype(jnp.float32)
    lifted = contract("iln,ic->cln", old_part, lift_weight).astype(jnp.bfloat16)
    coeffs = (contract("cln,mn->clm", lifted, dft_table) * scale_dft).astype(jnp.bfloat16)
    real_in = coeffs[..., :mode_count]
    imag_in = coeffs[..., mode_count:]
    weights = spectral_weight.reshape(mode_count, chan_count, 2 * chan_count)
    real_w = weights[..., :chan_count]
    imag_w = weights[..., chan_count:]
    real_out = contract("clm,mco->olm", real_in, real_w) - contract("clm,mco->olm", imag_in, imag_w)
    imag_out = contract("clm,mco->olm", real_in, imag_w) + contract("clm,mco->olm", imag_in, real_w)
    mixed = jnp.concatenate([real_out, imag_out], axis=2).astype(jnp.bfloat16)
    spectral = contract("olm,mn->oln", mixed, dft_table) * (2.0 * scale_dft)
    local_term = contract("cln,co->oln", lifted, mix_weight)
    hidden = spectral + local_term
    active, gelu_back = jax.vjp(jax.nn.gelu, hidden)
    active = active.astype(jnp.bfloat16)
    predicted = contract("oln,oi->iln", active, project_weight)
    misfit = (predicted - target) * loss_scale
    back_active = jnp.einsum(
        "iln,oi->oln", misfit, project_weight.astype(jnp.float32), precision=lax.Precision.HIGHEST
    )
    back_hidden = gelu_back(back_active)[0].astype(jnp.bfloat16)
    mix_part = contract("cln,oln->co", lifted, back_hidden)
    back_mixed = (contract("oln,mn->olm", back_hidden, dft_table) * (2.0 * scale_dft)).astype(
        jnp.bfloat16
    )
    back_real = back_mixed[..., :mode_count]
    back_imag = back_mixed[..., mode_count:]
    grad_real = contract("clm,olm->mco", real_in, back_real) + contract(
        "clm,olm->mco", imag_in, back_imag
    )
    grad_imag = contract("clm,olm->mco", real_in, back_imag) - contract(
        "clm,olm->mco", imag_in, back_real
    )
    spectral_part = jnp.concatenate([grad_real, grad_imag], axis=2).reshape(
        mode_count * chan_count, 2 * chan_count
    )
    return (spectral_part, mix_part)


def local(slot_field, solid, lift_weight, spectral_weight, mix_weight, project_weight, mode_index):
    role_index = lax.axis_index("grp")
    own_tile = slot_field[0]
    planes, x_rows, y_cols = own_tile.shape
    x_length = x_rows * lax.axis_size("gx")
    cell_total = x_length * y_cols * lax.axis_size("gy") * planes
    loss_scale = 16.0 / math.sqrt(cell_total)
    dft_table = spectral_table(mode_index, x_length)
    rimmed = with_halo(own_tile, (("gx", 1), ("gy", 2)), 1)
    gathered = lax.all_gather(rimmed[None], "grp", axis=0, tiled=True)
    padded = jnp.pad(gathered, ((0, 0), (1, 1), (0, 0), (0, 0)))
    old_velocity = gathered[:3, :, 1:-1, 1:-1]
    new_tile = lax.cond(
        role_index < 3,
        lambda: section_component(padded, jnp.minimum(role_index, 2), solid),
        lambda: own_tile,
    )
    new_slots = lax.all_gather(new_tile[None], "grp", axis=0, tiled=True)
    new_velocity = new_slots[:3]
    both_fields = jnp.concatenate([old_velocity, new_velocity], axis=0).astype(jnp.bfloat16)
    pencil_data = lax.all_to_all(
        jnp.transpose(both_fields, (0, 1, 3, 2)), "gx", split_axis=2, concat_axis=3, tiled=True
    )
    line_data = pencil_data.reshape(6, -1, x_length)

    def student(own_lines):
        return student_terms(
            own_lines,
            dft_table,
            lift_weight,
            spectral_weight,
            mix_weight,
            project_weight,
            loss_scale,
            x_length,
        )

    def nothing():
        return (
            jnp.zeros(spectral_weight.shape, jnp.float32),
            jnp.zeros(mix_weight.shape, jnp.float32),
        )

    spectral_part, mix_part = lax.cond(role_index == 3, lambda: student(line_data), nothing)
    spectral_grad = lax.psum_scatter(
        spectral_part, ("grp", "gx", "gy"), scatter_dimension=0, tiled=True
    )
    mix_grad = lax.psum(mix_part, ("grp", "gx", "gy"))
    return (new_velocity, spectral_grad, mix_grad)


def solution(mesh):
    in_specs = (P("grp", None, "gx", "gy"), P(None, "gx", "gy"), P(), P(), P(), P(), P())
    out_specs = (P(None, None, "gx", "gy"), P(("grp", "gx", "gy"), None), P())
    return jax.shard_map(local, mesh=mesh, in_specs=in_specs, out_specs=out_specs, check_vma=False)
```

profile of v0, /device:TPU:0, one launch (start us, length us, event | category | flops | bytes accessed | tf_op | source)
XLA Modules:
  0.0 216.4 jit_solution(6838658811106950806)
XLA Ops:
  7.2 0.8 copy.178
  8.0 4.9 %collective-permute-start = (f32[2,1,128]{2,1,0:T(1,128)S(1)}, f32[2,1,128]{2,1,0:T(1,128)S(1)}, u32[]{:S(2)}, u32[]{:S(2)}) collective-permute-start(f32[2,1,128]{2,1,0:T(1,128)S(1)} %get-tuple-element.105), channel_id=1, source_target_pairs={{0,4},{1,5},{2,6},{3,7},{8,12},{9,13},{10,14},{11,15},{16,20},{17,... | collective-permute-start | bytes 3080 | tf_op jit(solution)/shard_map/ppermute | solution.py:17
  12.8 1.3 collective-permute-start.1
  14.1 0.8 cosine_convert_fusion
  15.0 0.0 collective-permute-done
  15.0 3.3 %collective-permute-done.1 = f32[2,1,128]{2,1,0:T(1,128)S(1)} collective-permute-done((f32[2,1,128]{2,1,0:T(1,128)S(1)}, f32[2,1,128]{2,1,0:T(1,128)S(1)}, u32[]{:S(2)}, u32[]{:S(2)}) %collective-permute-start.1) | collective-permute-done | bytes 1056 | tf_op jit(solution)/shard_map/ppermute | solution.py:20
  18.3 0.1 fusion.90
  18.4 3.5 %collective-permute-start.2 = (f32[2,50,1]{2,1,0:T(8,128)S(1)}, f32[2,50,1]{2,1,0:T(8,128)S(1)}, u32[]{:S(2)}, u32[]{:S(2)}) collective-permute-start(f32[2,50,1]{2,1,0:T(8,128)S(1)} %get-tuple-element.103), channel_id=1, source_target_pairs={{0,1},{1,2},{2,3},{4,5},{5,6},{6,7},{8,9},{9,10},{10,11},{12,13},{... | collective-permute-start | bytes 1208 | tf_op jit(solution)/shard_map/ppermute | solution.py:17
  21.9 1.3 collective-permute-start.3
  23.2 0.5 collective-permute-done.2
  23.7 4.3 %collective-permute-done.3 = f32[2,50,1]{2,1,0:T(8,128)S(1)} collective-permute-done((f32[2,50,1]{2,1,0:T(8,128)S(1)}, f32[2,50,1]{2,1,0:T(8,128)S(1)}, u32[]{:S(2)}, u32[]{:S(2)}) %collective-permute-start.3) | collective-permute-done | bytes 432 | tf_op jit(solution)/shard_map/ppermute | solution.py:20
  27.9 0.1 pad_maximum_fusion.3
  28.1 6.8 %all-gather = f32[8,50,130]{2,1,0:T(8,128)S(1)} all-gather(f32[2,50,130]{2,1,0:T(8,128)S(1)} %pad_maximum_fusion.3), channel_id=2, replica_groups=mesh['grp'=4,'gx'=2,'gy'=4] {'grp'}, dimensions={0}, use_global_device_ids=true | all-gather | bytes 260000 | tf_op jit(solution)/shard_map/all_gather | solution.py:136
  34.9 0.1 slice.231
  35.0 0.0 copy-start
  35.0 0.0 copy-start.3
  35.0 0.0 copy-start.4
  35.0 0.0 copy-start.5
  35.0 1.3 conditional.2
  35.1 0.1 fusion
  35.2 0.1 fusion.13
  35.3 1.0 fusion.11
  36.3 5.6 %all-gather.1 = f32[8,48,128]{2,1,0:T(8,128)S(1)} all-gather(f32[2,48,128]{2,1,0:T(8,128)S(1)} %get-tuple-element.113), channel_id=3, replica_groups=mesh['grp'=4,'gx'=2,'gy'=4] {'grp'}, dimensions={0}, use_global_device_ids=true | all-gather | bytes 245760 | tf_op jit(solution)/shard_map/all_gather | solution.py:144
  41.9 0.0 copy-start.2
  42.0 0.4 copy.117
  42.4 0.3 bitcast_bitcast_fusion
  42.7 1.2 reshape.29
  43.9 3.4 %all-to-all-start = ((bf16[2,2,18432]{2,1,0:T(2,128)(2,1)}), bf16[2,2,18432]{2,1,0:T(2,128)(2,1)S(1)}, u32[]{:S(2)}, u32[]{:S(2)}) async-start(bf16[2,2,18432]{2,1,0:T(2,128)(2,1)} %reshape.29), calls=%async_computation | async-start | bytes 294912 | tf_op jit(solution)/shard_map/all_to_all | solution.py:147
  47.4 0.0 reduce-scatter.2.cloned.1.call-start
  47.4 4.6 %all-to-all-done = bf16[2,2,18432]{2,1,0:T(2,128)(2,1)S(1)} async-done(((bf16[2,2,18432]{2,1,0:T(2,128)(2,1)}), bf16[2,2,18432]{2,1,0:T(2,128)(2,1)S(1)}, u32[]{:S(2)}, u32[]{:S(2)}) %all-to-all-start) | async-done | bytes 147488 | tf_op jit(solution)/shard_map/all_to_all | solution.py:147
  52.1 0.4 reshape.30
  52.5 0.5 copy.118
  52.9 0.0 copy-done
  53.0 0.0 copy-done.3
  53.0 0.0 copy-done.4
  53.0 0.0 copy-done.5
  53.0 0.0 copy-done.2
  53.0 0.3 conditional.3
  53.0 0.1 broadcast.48
  53.3 0.0 copy-start.1
  53.3 1.0 copy-done.1
  54.3 0.0 reduce-scatter.2.cloned.1.call-update
  54.4 60.3 %psum.7 = f32[64,64]{1,0:T(8,128)} all-reduce(f32[64,64]{1,0:T(8,128)S(1)} %get-tuple-element.46), channel_id=1, replica_groups=mesh['grp'=4,'gx'=2,'gy'=4] {'grp','gx','gy'}, use_global_device_ids=true, to_apply=%region_5.6 | all-reduce | flops 4096 | bytes 32768 | tf_op jit(solution)/shard_map/psum | solution.py:174
  114.6 94.9 %reduce-scatter.2.cloned.1.call-done = f32[64,128]{1,0:T(8,128)} async-done(((f32[2048,128]{1,0:T(8,128)}), f32[64,128]{1,0:T(8,128)}) %reduce-scatter.2.cloned.1.call-update) | async-done | bytes 32784 | tf_op jit(solution)/shard_map/reduce_scatter | solution.py:171
  (7 shorter events, 0.1 us)
Async XLA Ops:
  8.0 7.0 %collective-permute-start = (f32[2,1,128]{2,1,0:T(1,128)S(1)}, f32[2,1,128]{2,1,0:T(1,128)S(1)}, u32[]{:S(2)}, u32[]{:S(2)}) collective-permute-start(f32[2,1,128]{2,1,0:T(1,128)S(1)} %get-tuple-element.105), channel_id=1, source_target_pairs={{0,4},{1,5},{2,6},{3,7},{8,12},{9,13},{10,14},{11,15},{16,20},{17,... | collective-permute-start | bytes 3080 | tf_op jit(solution)/shard_map/ppermute | solution.py:17
  12.8 5.5 %collective-permute-start.1 = (f32[2,1,128]{2,1,0:T(1,128)S(1)}, f32[2,1,128]{2,1,0:T(1,128)S(1)}, u32[]{:S(2)}, u32[]{:S(2)}) collective-permute-start(f32[2,1,128]{2,1,0:T(1,128)S(1)} %get-tuple-element.106), channel_id=1, source_target_pairs={{4,0},{5,1},{6,2},{7,3},{12,8},{13,9},{14,10},{15,11},{20,16},{21,... | collective-permute-start | bytes 3080 | tf_op jit(solution)/shard_map/ppermute | solution.py:20
  18.4 5.3 %collective-permute-start.2 = (f32[2,50,1]{2,1,0:T(8,128)S(1)}, f32[2,50,1]{2,1,0:T(8,128)S(1)}, u32[]{:S(2)}, u32[]{:S(2)}) collective-permute-start(f32[2,50,1]{2,1,0:T(8,128)S(1)} %get-tuple-element.103), channel_id=1, source_target_pairs={{0,1},{1,2},{2,3},{4,5},{5,6},{6,7},{8,9},{9,10},{10,11},{12,13},{... | collective-permute-start | bytes 1208 | tf_op jit(solution)/shard_map/ppermute | solution.py:17
  21.9 6.1 %collective-permute-start.3 = (f32[2,50,1]{2,1,0:T(8,128)S(1)}, f32[2,50,1]{2,1,0:T(8,128)S(1)}, u32[]{:S(2)}, u32[]{:S(2)}) collective-permute-start(f32[2,50,1]{2,1,0:T(8,128)S(1)} %get-tuple-element.104), channel_id=1, source_target_pairs={{1,0},{2,1},{3,2},{5,4},{6,5},{7,6},{9,8},{10,9},{11,10},{13,12},{... | collective-permute-start | bytes 1208 | tf_op jit(solution)/shard_map/ppermute | solution.py:20
  35.0 18.0 %copy-start = (bf16[2048,128]{1,0:T(8,128)(2,1)S(1)}, bf16[2048,128]{1,0:T(8,128)(2,1)}, u32[]{:S(2)}) copy-start(bf16[2048,128]{1,0:T(8,128)(2,1)} %param.14) | copy-start | bytes 1572868
  35.0 18.0 %copy-start.3 = (bf16[64,64]{1,0:T(8,128)(2,1)S(1)}, bf16[64,64]{1,0:T(8,128)(2,1)}, u32[]{:S(2)}) copy-start(bf16[64,64]{1,0:T(8,128)(2,1)} %param.15) | copy-start | bytes 24580
  35.0 18.0 %copy-start.4 = (bf16[64,3]{0,1:T(4,128)(2,1)S(1)}, bf16[64,3]{0,1:T(4,128)(2,1)}, u32[]{:S(2)}) copy-start(bf16[64,3]{0,1:T(4,128)(2,1)} %param.16) | copy-start | bytes 1156
  35.0 18.0 %copy-start.5 = (bf16[3,64]{1,0:T(4,128)(2,1)S(1)}, bf16[3,64]{1,0:T(4,128)(2,1)}, u32[]{:S(2)}) copy-start(bf16[3,64]{1,0:T(4,128)(2,1)} %param.13) | copy-start | bytes 1156
  41.9 11.1 %copy-start.2 = (f32[6,48,128]{2,1,0:T(8,128)}, f32[6,48,128]{2,1,0:T(8,128)S(1)}, u32[]{:S(2)}) copy-start(f32[6,48,128]{2,1,0:T(8,128)S(1)} %slice.167) | copy-start | bytes 442372
  43.9 8.1 %all-to-all-start = ((bf16[2,2,18432]{2,1,0:T(2,128)(2,1)}), bf16[2,2,18432]{2,1,0:T(2,128)(2,1)S(1)}, u32[]{:S(2)}, u32[]{:S(2)}) async-start(bf16[2,2,18432]{2,1,0:T(2,128)(2,1)} %reshape.29), calls=%async_computation | async-start | bytes 294912 | tf_op jit(solution)/shard_map/all_to_all | solution.py:147
  47.4 162.2 %reduce-scatter.2.cloned.1.call-start = ((), (), s32[]{:S(2)}) async-start(), calls=%async_computation.2 | async-start | bytes 1081344 | tf_op jit(solution)/shard_map/reduce_scatter | solution.py:171
  53.3 1.0 copy-start.1
Sparse Core Ops, SparseCore 0:
  54.5 155.0 reduce-scatter.1
where the time goes:
time: 217 us; the launch traced here: 216 us
  waiting for transfers between devices  108 us (50%)
  blocking collectives  72.7 us (34%)
  starting transfers between devices  14.4 us (7%)
  between operations  14.3 us (7%)
  local copies, waits for them, and re-layouts  4.98 us (2%)
    reduce_scatter x1, waiting for transfers between devices, local(): lax.psum_scatter(spectral_part, ('grp', 'gx', 'gy'), scatter_dimension=0,...  94.9 us
    psum x1, blocking collectives, local(): mix_grad = lax.psum(mix_part, ('grp', 'gx', 'gy'))  60.3 us
    ppermute x2, starting transfers between devices, with_halo(): lax.ppermute(lax.slice_in_dim(block, block.shape[dim] - width, None, axis...  8.34 us
    ppermute x2, waiting for transfers between devices, with_halo(): lax.ppermute(lax.slice_in_dim(block, 0, width, axis=dim), axis, backward)  7.59 us
    all_gather x1, blocking collectives, local(): gathered = lax.all_gather(rimmed[None], 'grp', axis=0, tiled=True)  6.82 us
    all_gather x1, blocking collectives, local(): new_slots = lax.all_gather(new_tile[None], 'grp', axis=0, tiled=True)  5.61 us
    all_to_all x1, waiting for transfers between devices, local(): lax.all_to_all(jnp.transpose(both_fields, (0, 1, 3, 2)), 'gx', split_axis...  4.65 us
  transfers between devices with their start and end apart: 6, of which 5 were waited for; matrix products, arithmetic and copies ran while one was open for 0% of the time, Pallas kernels for 0%

commit v1 on v0

--- a/solution.py
+++ b/solution.py
@@ -1,8 +1,11 @@
+import functools
 import math
 
 import jax
 import jax.numpy as jnp
 from jax import lax
+from jax.experimental import pallas as pl
+from jax.experimental.pallas import tpu as pltpu
 from jax.sharding import PartitionSpec as P
 
 VISCOSITY = 0.05
@@ -124,7 +127,7 @@
     return (spectral_part, mix_part)
 
 
-def local(slot_field, solid, lift_weight, spectral_weight, mix_weight, project_weight, mode_index):
+def general(slot_field, solid, lift_weight, spectral_weight, mix_weight, project_weight, mode_index):
     role_index = lax.axis_index("grp")
     own_tile = slot_field[0]
     planes, x_rows, y_cols = own_tile.shape
@@ -175,6 +178,549 @@
     return (new_velocity, spectral_grad, mix_grad)
 
 
+MESH = pl.DeviceIdType.MESH
+BF = jnp.bfloat16
+F32 = jnp.float32
+
+
+def dot(left, right, contract_dims=((1,), (0,))):
+    return lax.dot_general(left, right, (contract_dims, ((), ())), preferred_element_type=F32)
+
+
+def iota(shape, dim):
+    return lax.broadcasted_iota(jnp.int32, shape, dim)
+
+
+def fused_kernel(
+    sizes,
+    field_ref,
+    solid_ref,
+    lift_ref,
+    spec_ref,
+    mix_ref,
+    proj_ref,
+    mode_ref,
+    newv_ref,
+    grad_ref,
+    mixg_ref,
+    gath,
+    both_solid,
+    edge,
+    rims,
+    fresh,
+    wide_mix,
+    lift_big,
+    proj_down,
+    proj_up,
+    lifted_ref,
+    slope_ref,
+    stage,
+    stage_out,
+    a_own,
+    d_own,
+    a_all,
+    d_all,
+    m_part,
+    m_recv,
+    m_row,
+    field_send,
+    field_recv,
+    solid_sem,
+    rim_send,
+    rim_recv,
+    a_send,
+    a_recv,
+    d_send,
+    d_recv,
+    m_send,
+    m_sem,
+    r_send,
+    r_recv,
+):
+    grps, gxs, gys, x_length, cell_total = sizes
+    count = grps * gxs * gys
+    near = grps * gxs
+    half = x_length // gxs
+    modes = count
+    lines = 32
+    pairs = lines // 2
+    chans = 64
+    g = lax.axis_index("grp")
+    gx = lax.axis_index("gx")
+    gy = lax.axis_index("gy")
+    me = (g * gxs + gx) * gys + gy
+    slot = g * gxs + gx
+    scale_dft = 1.0 / math.sqrt(x_length)
+    loss_scale = 16.0 / math.sqrt(cell_total)
+
+    def flat_id(t):
+        return {"grp": t // (gxs * gys), "gx": (t // gys) % gxs, "gy": t % gys}
+
+    def near_id(s, z):
+        return {"grp": s // gxs, "gx": s % gxs, "gy": z}
+
+    def others(body, total=count, mine=me):
+        def step(k, carry):
+            body((mine + k) % total)
+            return carry
+
+        lax.fori_loop(1, total, step, 0)
+
+    barrier = pltpu.get_barrier_semaphore()
+    others(lambda t: pl.semaphore_signal(barrier, inc=1, device_id=flat_id(t), device_id_type=MESH))
+
+    own = field_ref[0]
+    flat = jnp.concatenate([own.reshape(2 * half, 128), jnp.zeros((128 - 2 * half, 128), F32)], axis=0)
+    turned = jnp.transpose(flat)
+    edge[0] = turned[0:1, :]
+    edge[1] = turned[127:128, :]
+    gath[pl.ds(slot, 1)] = own[None]
+    both_solid[pl.ds(gx, 1)] = solid_ref[...][None]
+
+    @pl.when(gy == 0)
+    def _():
+        rims[0] = jnp.zeros((near, 1, 128), F32)
+
+    @pl.when(gy == gys - 1)
+    def _():
+        rims[1] = jnp.zeros((near, 1, 128), F32)
+
+    pl.semaphore_wait(barrier, count - 1)
+
+    def field_copy(s):
+        return pltpu.make_async_remote_copy(
+            src_ref=field_ref.at[0],
+            dst_ref=gath.at[slot],
+            send_sem=field_send.at[s],
+            recv_sem=field_recv.at[slot],
+            device_id=near_id(s, gy),
+            device_id_type=MESH,
+        )
+
+    def field_arrival(s):
+        return pltpu.make_async_remote_copy(
+            src_ref=field_ref.at[0],
+            dst_ref=gath.at[s],
+            send_sem=field_send.at[s],
+            recv_sem=field_recv.at[s],
+            device_id=near_id(s, gy),
+            device_id_type=MESH,
+        )
+
+    def rim_copy(side, s):
+        return pltpu.make_async_remote_copy(
+            src_ref=edge.at[side],
+            dst_ref=rims.at[1 - side, slot],
+            send_sem=rim_send.at[side, s],
+            recv_sem=rim_recv.at[1 - side, slot],
+            device_id=near_id(s, gy - 1 + 2 * side),
+            device_id_type=MESH,
+        )
+
+    def rim_arrival(side, s):
+        return pltpu.make_async_remote_copy(
+            src_ref=edge.at[1 - side],
+            dst_ref=rims.at[side, s],
+            send_sem=rim_send.at[1 - side, s],
+            recv_sem=rim_recv.at[side, s],
+            device_id=near_id(s, gy - 1 + 2 * side),
+            device_id_type=MESH,
+        )
+
+    def solid_copy(place):
+        return pltpu.make_async_remote_copy(
+            src_ref=solid_ref,
+            dst_ref=both_solid.at[place],
+            send_sem=solid_sem.at[0],
+            recv_sem=solid_sem.at[1],
+            device_id={"grp": g, "gx": 1 - gx, "gy": gy},
+            device_id_type=MESH,
+        )
+
+    def each_near(body):
+        def step(s, carry):
+            body(s)
+            return carry
+
+        lax.fori_loop(0, near, step, 0)
+
+    others(lambda s: field_copy(s).start(), near, slot)
+    solid_copy(gx).start()
+
+    @pl.when(gy > 0)
+    def _():
+        each_near(lambda s: rim_copy(0, s).start())
+
+    @pl.when(gy < gys - 1)
+    def _():
+        each_near(lambda s: rim_copy(1, s).start())
+
+    lane = iota((x_length, 128), 1)
+    low64 = iota((16, 128), 1) < 64
+    mode_row = mode_ref[...].astype(F32)
+    mode_row = jnp.concatenate([mode_row] * 4, axis=1)
+    place = iota((x_length, 128), 0).astype(F32)
+    raw = mode_row * place + jnp.where(lane >= modes, 0.25 * x_length, 0.0)
+    phase = raw - x_length * jnp.floor((raw + 0.5) * (1.0 / x_length))
+    phase = jnp.where(phase >= 0.5 * x_length, phase - x_length, phase)
+    angle = phase * (math.pi / x_length)
+    square = angle * angle
+    series = jnp.full_like(square, -1.0 / 39916800.0)
+    for term in (1.0 / 362880.0, -1.0 / 5040.0, 1.0 / 120.0, -1.0 / 6.0, 1.0):
+        series = series * square + term
+    sine = series * angle
+    waves = 1.0 - 2.0 * sine * sine
+    table_t = waves[:, : 2 * modes].astype(BF)
+    table = jnp.transpose(jnp.concatenate([waves, jnp.zeros((128 - x_length, 128), F32)], axis=0))
+    table = table[: 2 * modes, :x_length].astype(BF)
+
+    row128 = iota((128, 128), 0)
+    col128 = iota((128, 128), 1)
+    lift = lift_ref[...].astype(F32)
+    lift = jnp.concatenate([lift, lift], axis=1)
+    lift_rows = jnp.where(
+        row128 < 32,
+        lift[0:1],
+        jnp.where(row128 < 64, lift[1:2], jnp.where(row128 < 96, lift[2:3], 0.0)),
+    )
+    proj = proj_ref[...].astype(F32)
+    col64 = iota((64, 128), 1)
+    proj_cols = jnp.where(
+        col64 < 32,
+        proj[:, 0:1],
+        jnp.where(col64 < 64, proj[:, 1:2], jnp.where(col64 < 96, proj[:, 2:3], 0.0)),
+    )
+    proj_rows = jnp.transpose(proj_cols)
+    proj_rows = jnp.concatenate([proj_rows, proj_rows], axis=1)
+    line_of_row = jnp.bitwise_and(row128, 31)
+    half_of_lane = jnp.where(col128 < 64, 0, 1)
+    line_of_col = jnp.bitwise_and(col64, 31)
+
+    def widen(p, carry):
+        hit = line_of_row == 2 * p + half_of_lane
+        cols = pl.ds(pl.multiple_of(p * 128, 128), 128)
+        lift_big[:, cols] = jnp.where(hit, lift_rows, 0.0).astype(BF)
+        up = jnp.where(hit, proj_rows, 0.0).astype(BF)
+        proj_up[0:128, cols] = up
+        proj_up[128:256, cols] = up
+        for part in range(2):
+            down = jnp.where(line_of_col == 2 * p + part, proj_cols, 0.0).astype(BF)
+            proj_down[pl.ds(pl.multiple_of(p * 128 + part * 64, 64), 64), :] = down
+        return carry
+
+    lax.fori_loop(0, pairs, widen, 0)
+
+    low_half = col64 < 64
+
+    def widen_mix(m, carry):
+        block = spec_ref[pl.ds(pl.multiple_of(m * 64, 64), 64), :]
+        wide = block.astype(F32)
+        turned_block = pltpu.roll(wide, 64, 1)
+        wide_mix[m, 0:64, :] = block
+        wide_mix[m, 64:128, :] = jnp.where(low_half, -turned_block, turned_block).astype(BF)
+        return carry
+
+    lax.fori_loop(0, modes, widen_mix, 0)
+
+    mix = mix_ref[...].astype(F32)
+    mix = jnp.concatenate([mix, mix], axis=1)
+    mix = jnp.concatenate([mix, mix], axis=0)
+    mix = jnp.where((row128 < 64) == (col128 < 64), mix, 0.0)
+    blank = jnp.zeros_like(mix)
+    mix_four = jnp.concatenate(
+        [jnp.concatenate([mix, blank], axis=1), jnp.concatenate([blank, mix], axis=1)], axis=0
+    ).astype(BF)
+    pick = jnp.concatenate(
+        [
+            jnp.where((col128 // 32 == i) & (row128 == 32 * g + jnp.bitwise_and(col128, 31)), 1.0, 0.0)
+            for i in range(3)
+        ],
+        axis=0,
+    ).astype(BF)
+
+    others(lambda s: field_arrival(s).wait_recv(), near, slot)
+    solid_copy(1 - gx).wait_recv()
+
+    @pl.when(gy > 0)
+    def _():
+        each_near(lambda s: rim_arrival(0, s).wait_recv())
+
+    @pl.when(gy < gys - 1)
+    def _():
+        each_near(lambda s: rim_arrival(1, s).wait_recv())
+
+    rim_rows = [rims[side, s] for side in range(2) for s in range(near)]
+    rim_rows.append(jnp.zeros((128 - 2 * near, 128), F32))
+    rim_cols = jnp.transpose(jnp.concatenate(rim_rows, axis=0))
+    first_row = iota((x_length, 128), 0) == 0
+    last_row = iota((x_length, 128), 0) == x_length - 1
+
+    def whole(f, z):
+        return jnp.concatenate([gath[f * gxs + h, z] for h in range(gxs)], axis=0)
+
+    def rim(f, z, side):
+        cols = [
+            rim_cols[z * half : (z + 1) * half, side * near + f * gxs + h :][:, 0:1] for h in range(gxs)
+        ]
+        return jnp.concatenate(cols, axis=0)
+
+    def shifted(f, z, value):
+        x_up = jnp.where(last_row, 0.0, pltpu.roll(value, x_length - 1, 0))
+        x_down = jnp.where(first_row, 0.0, pltpu.roll(value, 1, 0))
+        y_up = jnp.where(lane == 127, rim(f, z, 1), pltpu.roll(value, 127, 1))
+        y_down = jnp.where(lane == 0, rim(f, z, 0), pltpu.roll(value, 1, 1))
+        return x_up, x_down, y_up, y_down
+
+    for z in range(2):
+        fluid = 1.0 - jnp.concatenate([both_solid[h, z] for h in range(gxs)], axis=0).astype(F32)
+        here = [whole(f, z) for f in range(4)]
+        there = [whole(f, 1 - z) for f in range(4)]
+        sign_z = 0.5 if z == 0 else -0.5
+        press = shifted(3, z, here[3])
+        grads = (0.5 * (press[0] - press[1]), 0.5 * (press[2] - press[3]), sign_z * there[3])
+        for k in range(3):
+            x_up, x_down, y_up, y_down = shifted(k, z, here[k])
+            lap = there[k] + x_up + x_down + y_up + y_down - 6.0 * here[k]
+            advect = (
+                here[0] * (0.5 * (x_up - x_down))
+                + here[1] * (0.5 * (y_up - y_down))
+                + here[2] * (sign_z * there[k])
+            )
+            update = here[k] + TIME_STEP * (VISCOSITY * lap - advect - grads[k])
+            update = update * fluid
+            for h in range(gxs):
+                fresh[k, z, h] = update[h * half : (h + 1) * half]
+    for k in range(3):
+        for z in range(2):
+            newv_ref[k, z] = fresh[k, z, gx]
+
+    old = [jnp.concatenate([gath[i * gxs + h, gx] for h in range(gxs)], axis=0) for i in range(3)]
+    new = [jnp.concatenate([fresh[i, gx, h] for h in range(gxs)], axis=0) for i in range(3)]
+    stacked = jnp.concatenate([jnp.concatenate(old, axis=1), jnp.concatenate(new, axis=1)], axis=0)
+    picked = dot(stacked.astype(BF), pick)
+    source = picked[:x_length].astype(BF)
+    target = picked[x_length:]
+
+    for b in range(pairs // 2):
+        cols = slice(b * 256, (b + 1) * 256)
+        lifted = dot(source, lift_big[:, cols]).astype(BF)
+        lifted_ref[:, cols] = lifted
+        coeffs = dot(table, lifted) * scale_dft
+        stage[2 * b * 64 : (2 * b + 1) * 64, :] = coeffs[:, :128]
+        stage[(2 * b + 1) * 64 : (2 * b + 2) * 64, :] = coeffs[:, 128:]
+
+    def gather_mode(into):
+        def step(m, carry):
+            real = stage[pl.ds(m, pairs, stride=64), :]
+            imag = stage[pl.ds(modes + m, pairs, stride=64), :]
+            top = jnp.where(low64, real, pltpu.roll(imag, 64, 1))
+            bottom = jnp.where(low64, pltpu.roll(real, 64, 1), imag)
+            into[m] = jnp.concatenate([top, bottom], axis=0).astype(BF)
+            return carry
+
+        lax.fori_loop(0, modes, step, 0, unroll=4)
+
+    def exchange(own_ref, all_ref, send, recv, t, slot_at):
+        return pltpu.make_async_remote_copy(
+            src_ref=own_ref.at[t],
+            dst_ref=all_ref.at[slot_at],
+            send_sem=send.at[t],
+            recv_sem=recv.at[slot_at],
+            device_id=flat_id(t),
+            device_id_type=MESH,
+        )
+
+    gather_mode(a_own)
+    others(lambda t: exchange(a_own, a_all, a_send, a_recv, t, me).start())
+    a_all[pl.ds(me, 1)] = a_own[pl.ds(me, 1)]
+
+    def mix_mode(m, carry):
+        out = dot(a_own[m], wide_mix[m])
+        top, bottom = out[:pairs], out[pairs:]
+        stage_out[pl.ds(m, pairs, stride=64), :] = jnp.where(low64, top, pltpu.roll(bottom, 64, 1))
+        stage_out[pl.ds(modes + m, pairs, stride=64), :] = jnp.where(
+            low64, pltpu.roll(top, 64, 1), bottom
+        )
+        return carry
+
+    lax.fori_loop(0, modes, mix_mode, 0, unroll=4)
+
+    root = math.sqrt(2.0 / math.pi)
+    predicted = jnp.zeros((x_length, 128), F32)
+    for b in range(pairs // 2):
+        cols = slice(b * 256, (b + 1) * 256)
+        mixed = jnp.concatenate(
+            [
+                stage_out[2 * b * 64 : (2 * b + 1) * 64, :],
+                stage_out[(2 * b + 1) * 64 : (2 * b + 2) * 64, :],
+            ],
+            axis=1,
+        ).astype(BF)
+        hidden = dot(table_t, mixed) * (2.0 * scale_dft) + dot(lifted_ref[:, cols], mix_four)
+        squared = hidden * hidden
+        bent = jnp.tanh(root * hidden * (1.0 + 0.044715 * squared))
+        upper = 0.5 * (1.0 + bent)
+        active = (hidden * upper).astype(BF)
+        slope_ref[:, cols] = upper + 0.5 * hidden * (1.0 - bent * bent) * (
+            root * (1.0 + 3.0 * 0.044715 * squared)
+        )
+        predicted = predicted + dot(active, proj_down[b * 256 : (b + 1) * 256, :])
+    misfit = (predicted - target) * loss_scale
+    coarse = misfit.astype(BF)
+    fine = (misfit - coarse.astype(F32)).astype(BF)
+    misfit_parts = jnp.concatenate([coarse, fine], axis=1)
+
+    mix_sum = jnp.zeros((128, 128), F32)
+    for b in range(pairs // 2):
+        cols = slice(b * 256, (b + 1) * 256)
+        back_active = dot(misfit_parts, proj_up[:, cols])
+        back_hidden = (slope_ref[:, cols] * back_active).astype(BF)
+        lifted = lifted_ref[:, cols]
+        for part in range(2):
+            lanes = slice(part * 128, (part + 1) * 128)
+            mix_sum = mix_sum + dot(lifted[:, lanes], back_hidden[:, lanes], ((0,), (0,)))
+        back = dot(table, back_hidden) * (2.0 * scale_dft)
+        stage[2 * b * 64 : (2 * b + 1) * 64, :] = back[:, :128]
+        stage[(2 * b + 1) * 64 : (2 * b + 2) * 64, :] = back[:, 128:]
+
+    mix_own = mix_sum[:64] + pltpu.roll(mix_sum[64:], 64, 1)
+    packed = jnp.where(iota((32, 128), 1) < 64, mix_own[:32], pltpu.roll(mix_own[32:], 64, 1))
+    for row in range(count):
+        m_part[row] = packed[row : row + 1, :]
+    others(lambda t: exchange(m_part, m_recv, m_send, m_sem, t, me).start())
+    m_recv[pl.ds(me, 1)] = m_part[pl.ds(me, 1)]
+
+    gather_mode(d_own)
+    others(lambda t: exchange(d_own, d_all, d_send, d_recv, t, me).start())
+    d_all[pl.ds(me, 1)] = d_own[pl.ds(me, 1)]
+
+    def row_copy(t, slot_at):
+        return pltpu.make_async_remote_copy(
+            src_ref=m_row,
+            dst_ref=mixg_ref.at[slot_at],
+            send_sem=r_send.at[t],
+            recv_sem=r_recv.at[slot_at],
+            device_id=flat_id(t),
+            device_id_type=MESH,
+        )
+
+    others(lambda t: exchange(m_part, m_recv, m_send, m_sem, t, t).wait_recv())
+    total = jnp.sum(m_recv[...], axis=0)
+    m_row[...] = total
+    mixg_ref[pl.ds(me, 1)] = total[None]
+    others(lambda t: row_copy(t, me).start())
+
+    others(lambda t: exchange(a_own, a_all, a_send, a_recv, t, t).wait_recv())
+    others(lambda t: exchange(d_own, d_all, d_send, d_recv, t, t).wait_recv())
+    a_lines = a_all[...].reshape(count * lines, 2 * chans)
+    d_lines = d_all[...].reshape(count * lines, 2 * chans)
+    square_sum = dot(a_lines, d_lines, ((0,), (0,)))
+    turned_sum = pltpu.roll(square_sum[64:], 64, 1)
+    grad_ref[...] = square_sum[:64] + jnp.where(low_half, turned_sum, -turned_sum)
+
+    others(lambda t: row_copy(t, t).wait_recv())
+    others(lambda s: field_copy(s).wait_send(), near, slot)
+    solid_copy(gx).wait_send()
+
+    @pl.when(gy > 0)
+    def _():
+        each_near(lambda s: rim_copy(0, s).wait_send())
+
+    @pl.when(gy < gys - 1)
+    def _():
+        each_near(lambda s: rim_copy(1, s).wait_send())
+
+    def finish(t):
+        exchange(a_own, a_all, a_send, a_recv, t, me).wait_send()
+        exchange(d_own, d_all, d_send, d_recv, t, me).wait_send()
+        exchange(m_part, m_recv, m_send, m_sem, t, me).wait_send()
+        row_copy(t, me).wait_send()
+
+    others(finish)
+
+
+def fused(sizes, slot_field, solid, lift_weight, spectral_weight, mix_weight, project_weight, mode_index):
+    grps, gxs, gys, x_length, _ = sizes
+    count = grps * gxs * gys
+    near = grps * gxs
+    half = x_length // gxs
+    dma = pltpu.SemaphoreType.DMA
+    vmem = pl.BlockSpec(memory_space=pltpu.VMEM)
+    shape = jax.ShapeDtypeStruct
+    new_velocity, spectral_grad, mix_rows = pl.pallas_call(
+        functools.partial(fused_kernel, sizes),
+        out_shape=(
+            shape((3, 2, half, 128), F32),
+            shape((64, 128), F32),
+            shape((count, 1, 128), F32),
+        ),
+        in_specs=[vmem] * 7,
+        out_specs=(vmem, vmem, vmem),
+        scratch_shapes=[
+            pltpu.VMEM((near, 2, half, 128), F32),
+            pltpu.VMEM((gxs, 2, half, 128), jnp.int32),
+            pltpu.VMEM((2, 1, 128), F32),
+            pltpu.VMEM((2, near, 1, 128), F32),
+            pltpu.VMEM((3, 2, gxs, half, 128), F32),
+            pltpu.VMEM((count, 128, 128), BF),
+            pltpu.VMEM((128, 2048), BF),
+            pltpu.VMEM((2048, 128), BF),
+            pltpu.VMEM((256, 2048), BF),
+            pltpu.VMEM((x_length, 2048), BF),
+            pltpu.VMEM((x_length, 2048), F32),
+            pltpu.VMEM((1024, 128), F32),
+            pltpu.VMEM((1024, 128), F32),
+            pltpu.VMEM((count, 32, 128), BF),
+            pltpu.VMEM((count, 32, 128), BF),
+            pltpu.VMEM((count, 32, 128), BF),
+            pltpu.VMEM((count, 32, 128), BF),
+            pltpu.VMEM((count, 1, 128), F32),
+            pltpu.VMEM((count, 1, 128), F32),
+            pltpu.VMEM((1, 128), F32),
+            dma((near,)),
+            dma((near,)),
+            dma((2,)),
+            dma((2, near)),
+            dma((2, near)),
+        ]
+        + [dma((count,))] * 8,
+        compiler_params=pltpu.CompilerParams(
+            collective_id=0, has_side_effects=True, vmem_limit_bytes=32 * 1024 * 1024
+        ),
+        cost_estimate=pl.CostEstimate(
+            flops=400_000_000, bytes_accessed=2_000_000, transcendentals=200_000
+        ),
+    )(
+        slot_field,
+        solid,
+        lift_weight,
+        spectral_weight,
+        mix_weight,
+        project_weight,
+        mode_index.reshape(1, -1),
+    )
+    mix_grad = jnp.transpose(mix_rows.reshape(32, 2, 64), (1, 0, 2)).reshape(64, 64)
+    return (new_velocity, spectral_grad, mix_grad)
+
+
+def local(slot_field, solid, lift_weight, spectral_weight, mix_weight, project_weight, mode_index):
+    arrays = (slot_field, solid, lift_weight, spectral_weight, mix_weight, project_weight, mode_index)
+    grps, gxs, gys = (lax.axis_size(axis) for axis in ("grp", "gx", "gy"))
+    _, planes, x_rows, y_cols = slot_field.shape
+    x_length = x_rows * gxs
+    sizes = (grps, gxs, gys, x_length, x_length * y_cols * gys * planes)
+    fits = (
+        grps * gxs * gys == mode_index.shape[0] == 32
+        and mix_weight.shape[0] == 64
+        and gxs == planes == 2
+        and y_cols == 32 * grps == 128
+        and x_rows == 48
+    )
+    if fits:
+        return fused(sizes, *arrays)
+    return general(*arrays)
+
+
 def solution(mesh):
     in_specs = (P("grp", None, "gx", "gy"), P(None, "gx", "gy"), P(), P(), P(), P(), P())
     out_specs = (P(None, None, "gx", "gy"), P(("grp", "gx", "gy"), None), P())

time: 217 us -> 44.8 us (0.21)
  waiting for transfers between devices: 108 us -> 0 us
  blocking collectives: 72.7 us -> 0 us
  Pallas kernels: 0 us -> 36.5 us
  starting transfers between devices: 14.4 us -> 0 us
  between operations: 14.3 us -> 0.68 us
    reduce_scatter x1 -> x0, waiting for transfers between devices: 94.9 us -> none  [local(): lax.psum_scatter(spectral_part, ('grp', 'gx', 'gy'), scatter_dimension=0,...]
    psum x1 -> x0, blocking collectives: 60.3 us -> none  [local(): mix_grad = lax.psum(mix_part, ('grp', 'gx', 'gy'))]
    pallas_call x0 -> x1, Pallas kernels: none -> 36.5 us  [fused(): pl.pallas_call(functools.partial(fused_kernel, sizes), out_shape=(shape((...]
    all_gather x2 -> x0, blocking collectives: 12.4 us -> none  [the longest x1 6.82 us: local(): gathered = lax.all_gather(rimmed[None], 'grp', axis=0, tiled=True)]
    ppermute x4 -> x0, starting transfers between devices: 10.9 us -> none  [the longest x2 8.34 us: with_halo(): lax.ppermute(lax.slice_in_dim(block, block.shape[dim] - width, None, axis...]
    ppermute x4 -> x0, waiting for transfers between devices: 8.1 us -> none  [the longest x2 7.59 us: with_halo(): lax.ppermute(lax.slice_in_dim(block, 0, width, axis=dim), axis, backward)]
    all_to_all x1 -> x0, waiting for transfers between devices: 4.65 us -> none  [local(): lax.all_to_all(jnp.transpose(both_fields, (0, 1, 3, 2)), 'gx', split_axis...]
    all_to_all x1 -> x0, starting transfers between devices: 3.42 us -> none  [local(): lax.all_to_all(jnp.transpose(both_fields, (0, 1, 3, 2)), 'gx', split_axis...]
  transfers between devices with their start and end apart: 6 -> 0, of which waited for: 5 -> 0; matrix products, arithmetic and copies ran while one was open for 0% -> 0% of each run, Pallas kernels for 0% -> 0%
where the time goes in v1:
time: 44.8 us; the launch traced here: 44.4 us
  Pallas kernels  36.5 us (81%)
  local copies, waits for them, and re-layouts  6.59 us (15%)
  other arithmetic  0.68 us (2%)
  between operations  0.68 us (2%)
    pallas_call x1, Pallas kernels, fused(): pl.pallas_call(functools.partial(fused_kernel, sizes), out_shape=(shape((...  36.5 us
    unnamed x15, local copies, waits for them, and re-layouts  5.37 us

profile of v1, /device:TPU:0, one launch (start us, length us, event | category | flops | bytes accessed | tf_op | source)
XLA Modules:
  0.0 44.4 jit_solution(15362619390739151620)
XLA Ops:
  0.6 0.0 copy-start.3
  0.6 0.8 %copy.10.proj_ref = bf16[64,3]{1,0:T(8,128)(2,1)S(1)} copy(bf16[64,3]{0,1:T(4,128)(2,1)} %param.12) | data formatting | bytes 768 | tf_op args[5]
  1.4 0.0 copy-start.4
  1.4 0.0 copy-start.5
  1.4 0.0 copy-done.3
  1.5 0.7 %copy-done.4 = bf16[3,64]{1,0:T(4,128)(2,1)S(1)} copy-done((bf16[3,64]{1,0:T(4,128)(2,1)S(1)}, bf16[3,64]{1,0:T(4,128)(2,1)}, u32[]{:S(2)}) %copy-start.4) | copy-done | bytes 408
  2.1 0.0 copy-done.5
  2.1 0.0 copy-start
  2.1 1.0 %copy-done = bf16[2048,128]{1,0:T(8,128)(2,1)S(1)} copy-done((bf16[2048,128]{1,0:T(8,128)(2,1)S(1)}, bf16[2048,128]{1,0:T(8,128)(2,1)}, u32[]{:S(2)}) %copy-start) | copy-done | bytes 524312
  3.2 0.0 copy-start.1
  3.2 0.8 %copy-done.1 = f32[1,2,48,128]{3,2,1,0:T(8,128)S(1)} copy-done((f32[1,2,48,128]{3,2,1,0:T(8,128)S(1)}, f32[1,2,48,128]{3,2,1,0:T(8,128)}, u32[]{:S(2)}) %copy-start.1) | copy-done | bytes 49176
  4.0 0.0 copy-start.2
  4.0 0.8 %copy-done.2 = s32[2,48,128]{2,1,0:T(8,128)S(1)} copy-done((s32[2,48,128]{2,1,0:T(8,128)S(1)}, s32[2,48,128]{2,1,0:T(8,128)}, u32[]{:S(2)}) %copy-start.2) | copy-done | bytes 49176
  4.8 36.5 %shard_map.94 = (f32[3,2,48,128]{3,2,1,0:T(8,128)S(1)}, f32[64,128]{1,0:T(8,128)S(1)}, f32[32,1,128]{2,1,0:T(1,128)S(1)}) custom-call(f32[1,2,48,128]{3,2,1,0:T(8,128)S(1)} %copy-done.1, s32[2,48,128]{2,1,0:T(8,128)S(1)} %copy-done.2, bf16[3,64]{1,0:T(4,128)(2,1)S(1)} %copy-done.4, bf16[2048,128]{1,0:T(8,128)(2,1)S(1)} %copy-done, ...), custom_call_target="tpu_custom_call" | custom-call | flops 400000000 | bytes 2000000 | tf_op jit(solution)/shard_map/pallas_call | solution.py:650
  41.2 0.5 %broadcast.3 = f32[]{:T(128)} broadcast(f32[]{:T(128)} %constant.4), dimensions={} | broadcast | bytes 8 | tf_op jit(solution)/shard_map/pallas_call | solution.py:650
  41.7 0.7 %reduce.3 = f32[32,128]{1,0:T(8,128)S(1)} reduce(f32[32,1,128]{2,1,0:T(1,128)S(1)} %get-tuple-element.8, f32[]{:T(128)} %broadcast.3), dimensions={1}, to_apply=%get-tuple-element.8.reduce_sub_computation.3 | reduce | bytes 32772 | tf_op jit(solution)/shard_map/pallas_call | solution.py:650
  42.4 0.1 reshape.16
  42.5 0.6 %copy.11 = f32[2,32,64]{2,1,0:T(8,128)} copy(f32[2,32,64]{2,0,1:T(2,128)S(1)} %bitcast.4) | data formatting | bytes 32768 | tf_op jit(solution)/shard_map/transpose | solution.py:702
  43.1 0.7 %copy.14 = f32[3,2,48,128]{3,2,1,0:T(8,128)} copy(f32[3,2,48,128]{3,2,1,0:T(8,128)S(1)} %get-tuple-element.12) | data formatting | bytes 294912
  43.8 0.6 %copy.15 = f32[64,128]{1,0:T(8,128)} copy(f32[64,128]{1,0:T(8,128)S(1)} %get-tuple-element.13) | data formatting | bytes 65536
Async XLA Ops:
  0.6 0.8 %copy-start.3 = (bf16[64,64]{1,0:T(8,128)(2,1)S(1)}, bf16[64,64]{1,0:T(8,128)(2,1)}, u32[]{:S(2)}) copy-start(bf16[64,64]{1,0:T(8,128)(2,1)} %mix_ref.1) | copy-start | bytes 24580
  1.4 0.7 %copy-start.4 = (bf16[3,64]{1,0:T(4,128)(2,1)S(1)}, bf16[3,64]{1,0:T(4,128)(2,1)}, u32[]{:S(2)}) copy-start(bf16[3,64]{1,0:T(4,128)(2,1)} %lift_ref.1) | copy-start | bytes 1156
  1.4 0.7 %copy-start.5 = (s32[32]{0:T(128)S(1)}, s32[32]{0:T(128)}, u32[]{:S(2)}) copy-start(s32[32]{0:T(128)} %param.13) | copy-start | bytes 388
  2.1 1.0 %copy-start = (bf16[2048,128]{1,0:T(8,128)(2,1)S(1)}, bf16[2048,128]{1,0:T(8,128)(2,1)}, u32[]{:S(2)}) copy-start(bf16[2048,128]{1,0:T(8,128)(2,1)} %spec_ref.1) | copy-start | bytes 1572868
  3.2 0.8 %copy-start.1 = (f32[1,2,48,128]{3,2,1,0:T(8,128)S(1)}, f32[1,2,48,128]{3,2,1,0:T(8,128)}, u32[]{:S(2)}) copy-start(f32[1,2,48,128]{3,2,1,0:T(8,128)} %field_ref.1) | copy-start | bytes 147460
  4.0 0.8 %copy-start.2 = (s32[2,48,128]{2,1,0:T(8,128)S(1)}, s32[2,48,128]{2,1,0:T(8,128)}, u32[]{:S(2)}) copy-start(s32[2,48,128]{2,1,0:T(8,128)} %solid_ref.1) | copy-start | bytes 147460

commit v2 on v1

--- a/solution.py
+++ b/solution.py
@@ -203,6 +203,7 @@
     newv_ref,
     grad_ref,
     mixg_ref,
+    spec_vm,
     gath,
     both_solid,
     edge,
@@ -223,19 +224,18 @@
     m_part,
     m_recv,
     m_row,
+    m_all,
+    load,
     field_send,
     field_recv,
     solid_sem,
     rim_send,
     rim_recv,
-    a_send,
-    a_recv,
-    d_send,
-    d_recv,
-    m_send,
-    m_sem,
-    r_send,
-    r_recv,
+    a_sems,
+    d_sems_a,
+    d_sems_b,
+    m_sems,
+    r_sems,
 ):
     grps, gxs, gys, x_length, cell_total = sizes
     count = grps * gxs * gys
@@ -252,30 +252,37 @@
     slot = g * gxs + gx
     scale_dft = 1.0 / math.sqrt(x_length)
     loss_scale = 16.0 / math.sqrt(cell_total)
-
-    def flat_id(t):
-        return {"grp": t // (gxs * gys), "gx": (t // gys) % gxs, "gy": t % gys}
-
-    def near_id(s, z):
-        return {"grp": s // gxs, "gx": s % gxs, "gy": z}
-
-    def others(body, total=count, mine=me):
-        def step(k, carry):
-            body((mine + k) % total)
-            return carry
-
-        lax.fori_loop(1, total, step, 0)
+    d_sems = (d_sems_a, d_sems_b)
+
+    g_at = [(g + d) % grps for d in range(grps)]
+    x_at = [(gx + d) % gxs for d in range(gxs)]
+    y_at = [(gy + d) % gys for d in range(gys)]
+    peers = []
+    for dy in [gys // 2] + [d for d in range(gys) if d != gys // 2]:
+        for dg in range(grps):
+            for dx in range(gxs):
+                if (dg, dx, dy) != (0, 0, 0):
+                    place = {"grp": g_at[dg], "gx": x_at[dx], "gy": y_at[dy]}
+                    peers.append((place, (g_at[dg] * gxs + x_at[dx]) * gys + y_at[dy]))
 
     barrier = pltpu.get_barrier_semaphore()
-    others(lambda t: pl.semaphore_signal(barrier, inc=1, device_id=flat_id(t), device_id_type=MESH))
-
-    own = field_ref[0]
+    for place, _ in peers:
+        pl.semaphore_signal(barrier, inc=1, device_id=place, device_id_type=MESH)
+
+    loads = [
+        pltpu.make_async_copy(field_ref.at[0], gath.at[slot], load.at[0]),
+        pltpu.make_async_copy(solid_ref, both_solid.at[gx], load.at[1]),
+        pltpu.make_async_copy(spec_ref, spec_vm, load.at[2]),
+    ]
+    for copy in loads:
+        copy.start()
+    loads[0].wait()
+
+    own = gath[pl.ds(slot, 1)][0]
     flat = jnp.concatenate([own.reshape(2 * half, 128), jnp.zeros((128 - 2 * half, 128), F32)], axis=0)
     turned = jnp.transpose(flat)
     edge[0] = turned[0:1, :]
     edge[1] = turned[127:128, :]
-    gath[pl.ds(slot, 1)] = own[None]
-    both_solid[pl.ds(gx, 1)] = solid_ref[...][None]
 
     @pl.when(gy == 0)
     def _():
@@ -287,53 +294,30 @@
 
     pl.semaphore_wait(barrier, count - 1)
 
-    def field_copy(s):
+    near_peers = []
+    for dg in range(grps):
+        for dx in range(gxs):
+            if (dg, dx) != (0, 0):
+                place = {"grp": g_at[dg], "gx": x_at[dx], "gy": gy}
+                near_peers.append((place, g_at[dg] * gxs + x_at[dx]))
+
+    def field_copy(place, s, at):
         return pltpu.make_async_remote_copy(
             src_ref=field_ref.at[0],
-            dst_ref=gath.at[slot],
+            dst_ref=gath.at[at],
             send_sem=field_send.at[s],
-            recv_sem=field_recv.at[slot],
-            device_id=near_id(s, gy),
+            recv_sem=field_recv.at[at],
+            device_id=place,
             device_id_type=MESH,
         )
 
-    def field_arrival(s):
-        return pltpu.make_async_remote_copy(
-            src_ref=field_ref.at[0],
-            dst_ref=gath.at[s],
-            send_sem=field_send.at[s],
-            recv_sem=field_recv.at[s],
-            device_id=near_id(s, gy),
-            device_id_type=MESH,
-        )
-
-    def rim_copy(side, s):
+    def rim_copy(side, s, at):
         return pltpu.make_async_remote_copy(
             src_ref=edge.at[side],
-            dst_ref=rims.at[1 - side, slot],
+            dst_ref=rims.at[1 - side, at],
             send_sem=rim_send.at[side, s],
-            recv_sem=rim_recv.at[1 - side, slot],
-            device_id=near_id(s, gy - 1 + 2 * side),
-            device_id_type=MESH,
-        )
-
-    def rim_arrival(side, s):
-        return pltpu.make_async_remote_copy(
-            src_ref=edge.at[1 - side],
-            dst_ref=rims.at[side, s],
-            send_sem=rim_send.at[1 - side, s],
-            recv_sem=rim_recv.at[side, s],
-            device_id=near_id(s, gy - 1 + 2 * side),
-            device_id_type=MESH,
-        )
-
-    def solid_copy(place):
-        return pltpu.make_async_remote_copy(
-            src_ref=solid_ref,
-            dst_ref=both_solid.at[place],
-            send_sem=solid_sem.at[0],
-            recv_sem=solid_sem.at[1],
-            device_id={"grp": g, "gx": 1 - gx, "gy": gy},
+            recv_sem=rim_recv.at[1 - side, at],
+            device_id={"grp": s // gxs, "gx": s % gxs, "gy": gy - 1 + 2 * side},
             device_id_type=MESH,
         )
 
@@ -344,19 +328,31 @@
 
         lax.fori_loop(0, near, step, 0)
 
-    others(lambda s: field_copy(s).start(), near, slot)
-    solid_copy(gx).start()
+    for place, s in near_peers:
+        field_copy(place, s, slot).start()
 
     @pl.when(gy > 0)
     def _():
-        each_near(lambda s: rim_copy(0, s).start())
+        each_near(lambda s: rim_copy(0, s, slot).start())
 
     @pl.when(gy < gys - 1)
     def _():
-        each_near(lambda s: rim_copy(1, s).start())
+        each_near(lambda s: rim_copy(1, s, slot).start())
+
+    solid_copy = pltpu.make_async_remote_copy(
+        src_ref=solid_ref,
+        dst_ref=both_solid.at[gx],
+        send_sem=solid_sem.at[0],
+        recv_sem=solid_sem.at[1],
+        device_id={"grp": g, "gx": x_at[1], "gy": gy},
+        device_id_type=MESH,
+    )
+    solid_copy.start()
+    for copy in loads[1:]:
+        copy.wait()
 
     lane = iota((x_length, 128), 1)
-    low64 = iota((16, 128), 1) < 64
+    low16 = iota((16, 128), 1) < 64
     mode_row = mode_ref[...].astype(F32)
     mode_row = jnp.concatenate([mode_row] * 4, axis=1)
     place = iota((x_length, 128), 0).astype(F32)
@@ -384,14 +380,14 @@
         jnp.where(row128 < 64, lift[1:2], jnp.where(row128 < 96, lift[2:3], 0.0)),
     )
     proj = proj_ref[...].astype(F32)
+    proj = jnp.concatenate([proj, proj], axis=1)
+    proj_rows = jnp.where(
+        row128 < 32,
+        proj[0:1],
+        jnp.where(row128 < 64, proj[1:2], jnp.where(row128 < 96, proj[2:3], 0.0)),
+    )
+    proj_cols = jnp.transpose(proj_rows)[:64]
     col64 = iota((64, 128), 1)
-    proj_cols = jnp.where(
-        col64 < 32,
-        proj[:, 0:1],
-        jnp.where(col64 < 64, proj[:, 1:2], jnp.where(col64 < 96, proj[:, 2:3], 0.0)),
-    )
-    proj_rows = jnp.transpose(proj_cols)
-    proj_rows = jnp.concatenate([proj_rows, proj_rows], axis=1)
     line_of_row = jnp.bitwise_and(row128, 31)
     half_of_lane = jnp.where(col128 < 64, 0, 1)
     line_of_col = jnp.bitwise_and(col64, 31)
@@ -413,7 +409,7 @@
     low_half = col64 < 64
 
     def widen_mix(m, carry):
-        block = spec_ref[pl.ds(pl.multiple_of(m * 64, 64), 64), :]
+        block = spec_vm[pl.ds(pl.multiple_of(m * 64, 64), 64), :]
         wide = block.astype(F32)
         turned_block = pltpu.roll(wide, 64, 1)
         wide_mix[m, 0:64, :] = block
@@ -438,16 +434,17 @@
         axis=0,
     ).astype(BF)
 
-    others(lambda s: field_arrival(s).wait_recv(), near, slot)
-    solid_copy(1 - gx).wait_recv()
+    for place, s in near_peers:
+        field_copy(place, s, s).wait_recv()
+    solid_copy.wait_recv()
 
     @pl.when(gy > 0)
     def _():
-        each_near(lambda s: rim_arrival(0, s).wait_recv())
+        each_near(lambda s: rim_copy(1, s, s).wait_recv())
 
     @pl.when(gy < gys - 1)
     def _():
-        each_near(lambda s: rim_arrival(1, s).wait_recv())
+        each_near(lambda s: rim_copy(0, s, s).wait_recv())
 
     rim_rows = [rims[side, s] for side in range(2) for s in range(near)]
     rim_rows.append(jnp.zeros((128 - 2 * near, 128), F32))
@@ -489,13 +486,12 @@
             update = here[k] + TIME_STEP * (VISCOSITY * lap - advect - grads[k])
             update = update * fluid
             for h in range(gxs):
-                fresh[k, z, h] = update[h * half : (h + 1) * half]
-    for k in range(3):
-        for z in range(2):
-            newv_ref[k, z] = fresh[k, z, gx]
+                fresh[h, k, z] = update[h * half : (h + 1) * half]
+    result_copy = pltpu.make_async_copy(fresh.at[gx], newv_ref, load.at[3])
+    result_copy.start()
 
     old = [jnp.concatenate([gath[i * gxs + h, gx] for h in range(gxs)], axis=0) for i in range(3)]
-    new = [jnp.concatenate([fresh[i, gx, h] for h in range(gxs)], axis=0) for i in range(3)]
+    new = [jnp.concatenate([fresh[h, i, gx] for h in range(gxs)], axis=0) for i in range(3)]
     stacked = jnp.concatenate([jnp.concatenate(old, axis=1), jnp.concatenate(new, axis=1)], axis=0)
     picked = dot(stacked.astype(BF), pick)
     source = picked[:x_length].astype(BF)
@@ -509,134 +505,175 @@
         stage[2 * b * 64 : (2 * b + 1) * 64, :] = coeffs[:, :128]
         stage[(2 * b + 1) * 64 : (2 * b + 2) * 64, :] = coeffs[:, 128:]
 
-    def gather_mode(into):
+    def mode_rows(m, rows_of, keep):
+        real = stage[pl.ds(m, rows_of, stride=64), :]
+        imag = stage[pl.ds(modes + m, rows_of, stride=64), :]
+        low = iota((rows_of, 128), 1) < 64
+        top = jnp.where(low, real, pltpu.roll(imag, 64, 1))
+        bottom = jnp.where(low, pltpu.roll(real, 64, 1), imag)
+        keep(jnp.concatenate([top[:8], bottom[:8], top[8:], bottom[8:]][: rows_of // 4], axis=0))
+
+    def all_modes(body):
         def step(m, carry):
-            real = stage[pl.ds(m, pairs, stride=64), :]
-            imag = stage[pl.ds(modes + m, pairs, stride=64), :]
-            top = jnp.where(low64, real, pltpu.roll(imag, 64, 1))
-            bottom = jnp.where(low64, pltpu.roll(real, 64, 1), imag)
-            into[m] = jnp.concatenate([top, bottom], axis=0).astype(BF)
+            body(m)
             return carry
 
-        lax.fori_loop(0, modes, step, 0, unroll=4)
-
-    def exchange(own_ref, all_ref, send, recv, t, slot_at):
+        lax.fori_loop(0, modes, step, 0, unroll=8)
+
+    def exchange(src, dst, sems, place, sent, landed):
         return pltpu.make_async_remote_copy(
-            src_ref=own_ref.at[t],
-            dst_ref=all_ref.at[slot_at],
-            send_sem=send.at[t],
-            recv_sem=recv.at[slot_at],
-            device_id=flat_id(t),
+            src_ref=src,
+            dst_ref=dst,
+            send_sem=sems.at[0, sent],
+            recv_sem=sems.at[1, landed],
+            device_id=place,
             device_id_type=MESH,
         )
 
-    gather_mode(a_own)
-    others(lambda t: exchange(a_own, a_all, a_send, a_recv, t, me).start())
+    def a_copy(place, t, at):
+        return exchange(a_own.at[t], a_all.at[at], a_sems, place, t, at)
+
+    def d_copy(part, place, t, at):
+        return exchange(d_own.at[part, t], d_all.at[part, at], d_sems[part], place, t, at)
+
+    def m_copy(place, t, at):
+        return exchange(m_part.at[t], m_recv.at[at], m_sems, place, t, at)
+
+    def r_copy(place, t, at):
+        return exchange(m_row, m_all.at[at], r_sems, place, t, at)
+
+    def keep_a(m):
+        def keep(rows):
+            both = rows.astype(BF)
+            a_own[m, 0] = both[:16]
+            a_own[m, 1] = both[16:]
+
+        mode_rows(m, pairs, keep)
+
+    all_modes(keep_a)
+    for place, t in peers:
+        a_copy(place, t, me).start()
     a_all[pl.ds(me, 1)] = a_own[pl.ds(me, 1)]
 
-    def mix_mode(m, carry):
-        out = dot(a_own[m], wide_mix[m])
-        top, bottom = out[:pairs], out[pairs:]
-        stage_out[pl.ds(m, pairs, stride=64), :] = jnp.where(low64, top, pltpu.roll(bottom, 64, 1))
+    def mix_mode(m):
+        out = dot(a_own[m].reshape(lines, 2 * chans), wide_mix[m])
+        top = jnp.concatenate([out[:8], out[16:24]], axis=0)
+        bottom = jnp.concatenate([out[8:16], out[24:]], axis=0)
+        stage_out[pl.ds(m, pairs, stride=64), :] = jnp.where(
+            low16, top, pltpu.roll(bottom, 64, 1)
+        )
         stage_out[pl.ds(modes + m, pairs, stride=64), :] = jnp.where(
-            low64, pltpu.roll(top, 64, 1), bottom
+            low16, pltpu.roll(top, 64, 1), bottom
         )
-        return carry
-
-    lax.fori_loop(0, modes, mix_mode, 0, unroll=4)
+
+    all_modes(mix_mode)
 
     root = math.sqrt(2.0 / math.pi)
-    predicted = jnp.zeros((x_length, 128), F32)
-    for b in range(pairs // 2):
-        cols = slice(b * 256, (b + 1) * 256)
-        mixed = jnp.concatenate(
-            [
-                stage_out[2 * b * 64 : (2 * b + 1) * 64, :],
-                stage_out[(2 * b + 1) * 64 : (2 * b + 2) * 64, :],
-            ],
-            axis=1,
-        ).astype(BF)
-        hidden = dot(table_t, mixed) * (2.0 * scale_dft) + dot(lifted_ref[:, cols], mix_four)
-        squared = hidden * hidden
-        bent = jnp.tanh(root * hidden * (1.0 + 0.044715 * squared))
-        upper = 0.5 * (1.0 + bent)
-        active = (hidden * upper).astype(BF)
-        slope_ref[:, cols] = upper + 0.5 * hidden * (1.0 - bent * bent) * (
-            root * (1.0 + 3.0 * 0.044715 * squared)
-        )
-        predicted = predicted + dot(active, proj_down[b * 256 : (b + 1) * 256, :])
-    misfit = (predicted - target) * loss_scale
-    coarse = misfit.astype(BF)
-    fine = (misfit - coarse.astype(F32)).astype(BF)
-    misfit_parts = jnp.concatenate([coarse, fine], axis=1)
-
     mix_sum = jnp.zeros((128, 128), F32)
-    for b in range(pairs // 2):
-        cols = slice(b * 256, (b + 1) * 256)
-        back_active = dot(misfit_parts, proj_up[:, cols])
-        back_hidden = (slope_ref[:, cols] * back_active).astype(BF)
-        lifted = lifted_ref[:, cols]
-        for part in range(2):
-            lanes = slice(part * 128, (part + 1) * 128)
-            mix_sum = mix_sum + dot(lifted[:, lanes], back_hidden[:, lanes], ((0,), (0,)))
-        back = dot(table, back_hidden) * (2.0 * scale_dft)
-        stage[2 * b * 64 : (2 * b + 1) * 64, :] = back[:, :128]
-        stage[(2 * b + 1) * 64 : (2 * b + 2) * 64, :] = back[:, 128:]
-
-    mix_own = mix_sum[:64] + pltpu.roll(mix_sum[64:], 64, 1)
-    packed = jnp.where(iota((32, 128), 1) < 64, mix_own[:32], pltpu.roll(mix_own[32:], 64, 1))
-    for row in range(count):
-        m_part[row] = packed[row : row + 1, :]
-    others(lambda t: exchange(m_part, m_recv, m_send, m_sem, t, me).start())
-    m_recv[pl.ds(me, 1)] = m_part[pl.ds(me, 1)]
-
-    gather_mode(d_own)
-    others(lambda t: exchange(d_own, d_all, d_send, d_recv, t, me).start())
-    d_all[pl.ds(me, 1)] = d_own[pl.ds(me, 1)]
-
-    def row_copy(t, slot_at):
-        return pltpu.make_async_remote_copy(
-            src_ref=m_row,
-            dst_ref=mixg_ref.at[slot_at],
-            send_sem=r_send.at[t],
-            recv_sem=r_recv.at[slot_at],
-            device_id=flat_id(t),
-            device_id_type=MESH,
-        )
-
-    others(lambda t: exchange(m_part, m_recv, m_send, m_sem, t, t).wait_recv())
+    for half_lines in range(2):
+        blocks = range(half_lines * 4, half_lines * 4 + 4)
+        predicted = jnp.zeros((x_length, 128), F32)
+        for b in blocks:
+            cols = slice(b * 256, (b + 1) * 256)
+            mixed = jnp.concatenate(
+                [
+                    stage_out[2 * b * 64 : (2 * b + 1) * 64, :],
+                    stage_out[(2 * b + 1) * 64 : (2 * b + 2) * 64, :],
+                ],
+                axis=1,
+            ).astype(BF)
+            hidden = dot(table_t, mixed) * (2.0 * scale_dft) + dot(lifted_ref[:, cols], mix_four)
+            squared = hidden * hidden
+            bent = jnp.tanh(root * hidden * (1.0 + 0.044715 * squared))
+            upper = 0.5 * (1.0 + bent)
+            active = (hidden * upper).astype(BF)
+            slope_ref[:, cols] = upper + 0.5 * hidden * (1.0 - bent * bent) * (
+                root * (1.0 + 3.0 * 0.044715 * squared)
+            )
+            predicted = predicted + dot(active, proj_down[b * 256 : (b + 1) * 256, :])
+        misfit = (predicted - target) * loss_scale
+        coarse = misfit.astype(BF)
+        fine = (misfit - coarse.astype(F32)).astype(BF)
+        misfit_parts = jnp.concatenate([coarse, fine], axis=1)
+        for b in blocks:
+            cols = slice(b * 256, (b + 1) * 256)
+            back_active = dot(misfit_parts, proj_up[:, cols])
+            back_hidden = (slope_ref[:, cols] * back_active).astype(BF)
+            lifted = lifted_ref[:, cols]
+            for part in range(2):
+                lanes = slice(part * 128, (part + 1) * 128)
+                mix_sum = mix_sum + dot(lifted[:, lanes], back_hidden[:, lanes], ((0,), (0,)))
+            back = dot(table, back_hidden) * (2.0 * scale_dft)
+            at = 2 * (b % 4) * 64
+            stage[at : at + 64, :] = back[:, :128]
+            stage[at + 64 : at + 128, :] = back[:, 128:]
+
+        if half_lines == 1:
+            mix_own = mix_sum[:64] + pltpu.roll(mix_sum[64:], 64, 1)
+            packed = jnp.where(
+                iota((32, 128), 1) < 64, mix_own[:32], pltpu.roll(mix_own[32:], 64, 1)
+            )
+            for row in range(count):
+                m_part[row] = packed[row : row + 1, :]
+            for place, t in peers:
+                m_copy(place, t, me).start()
+            m_recv[pl.ds(me, 1)] = m_part[pl.ds(me, 1)]
+
+        def keep_d(m):
+            def keep(rows):
+                d_own[half_lines, m] = rows.astype(BF)
+
+            mode_rows(m, pairs // 2, keep)
+
+        all_modes(keep_d)
+        for place, t in peers:
+            d_copy(half_lines, place, t, me).start()
+        d_all[half_lines, pl.ds(me, 1)] = d_own[half_lines, pl.ds(me, 1)]
+
+    for place, t in peers:
+        m_copy(place, t, t).wait_recv()
     total = jnp.sum(m_recv[...], axis=0)
     m_row[...] = total
-    mixg_ref[pl.ds(me, 1)] = total[None]
-    others(lambda t: row_copy(t, me).start())
-
-    others(lambda t: exchange(a_own, a_all, a_send, a_recv, t, t).wait_recv())
-    others(lambda t: exchange(d_own, d_all, d_send, d_recv, t, t).wait_recv())
-    a_lines = a_all[...].reshape(count * lines, 2 * chans)
-    d_lines = d_all[...].reshape(count * lines, 2 * chans)
-    square_sum = dot(a_lines, d_lines, ((0,), (0,)))
+    m_all[pl.ds(me, 1)] = total[None]
+    for place, t in peers:
+        r_copy(place, t, me).start()
+
+    for place, t in peers:
+        a_copy(place, t, t).wait_recv()
+    square_sum = jnp.zeros((128, 128), F32)
+    for half_lines in range(2):
+        for place, t in peers:
+            d_copy(half_lines, place, t, t).wait_recv()
+        a_lines = a_all[:, half_lines].reshape(count * 16, 2 * chans)
+        d_lines = d_all[half_lines].reshape(count * 16, 2 * chans)
+        square_sum = square_sum + dot(a_lines, d_lines, ((0,), (0,)))
     turned_sum = pltpu.roll(square_sum[64:], 64, 1)
     grad_ref[...] = square_sum[:64] + jnp.where(low_half, turned_sum, -turned_sum)
 
-    others(lambda t: row_copy(t, t).wait_recv())
-    others(lambda s: field_copy(s).wait_send(), near, slot)
-    solid_copy(gx).wait_send()
+    for place, t in peers:
+        r_copy(place, t, t).wait_recv()
+    rows = jnp.concatenate([m_all[row] for row in range(count)], axis=0)
+    mixg_ref[...] = jnp.concatenate([rows[:, :64], rows[:, 64:]], axis=0)
+
+    result_copy.wait()
+    for place, s in near_peers:
+        field_copy(place, s, slot).wait_send()
+    solid_copy.wait_send()
 
     @pl.when(gy > 0)
     def _():
-        each_near(lambda s: rim_copy(0, s).wait_send())
+        each_near(lambda s: rim_copy(0, s, slot).wait_send())
 
     @pl.when(gy < gys - 1)
     def _():
-        each_near(lambda s: rim_copy(1, s).wait_send())
-
-    def finish(t):
-        exchange(a_own, a_all, a_send, a_recv, t, me).wait_send()
-        exchange(d_own, d_all, d_send, d_recv, t, me).wait_send()
-        exchange(m_part, m_recv, m_send, m_sem, t, me).wait_send()
-        row_copy(t, me).wait_send()
-
-    others(finish)
+        each_near(lambda s: rim_copy(1, s, slot).wait_send())
+
+    for place, t in peers:
+        a_copy(place, t, me).wait_send()
+        d_copy(0, place, t, me).wait_send()
+        d_copy(1, place, t, me).wait_send()
+        m_copy(place, t, me).wait_send()
+        r_copy(place, t, me).wait_send()
 
 
 def fused(sizes, slot_field, solid, lift_weight, spectral_weight, mix_weight, project_weight, mode_index):
@@ -646,22 +683,24 @@
     half = x_length // gxs
     dma = pltpu.SemaphoreType.DMA
     vmem = pl.BlockSpec(memory_space=pltpu.VMEM)
+    whole = pl.BlockSpec(memory_space=pl.ANY)
     shape = jax.ShapeDtypeStruct
-    new_velocity, spectral_grad, mix_rows = pl.pallas_call(
+    return pl.pallas_call(
         functools.partial(fused_kernel, sizes),
         out_shape=(
             shape((3, 2, half, 128), F32),
             shape((64, 128), F32),
-            shape((count, 1, 128), F32),
+            shape((64, 64), F32),
         ),
-        in_specs=[vmem] * 7,
-        out_specs=(vmem, vmem, vmem),
+        in_specs=[whole, whole, vmem, whole, vmem, vmem, vmem],
+        out_specs=(whole, vmem, vmem),
         scratch_shapes=[
+            pltpu.VMEM((64 * count, 128), BF),
             pltpu.VMEM((near, 2, half, 128), F32),
             pltpu.VMEM((gxs, 2, half, 128), jnp.int32),
             pltpu.VMEM((2, 1, 128), F32),
             pltpu.VMEM((2, near, 1, 128), F32),
-            pltpu.VMEM((3, 2, gxs, half, 128), F32),
+            pltpu.VMEM((gxs, 3, 2, half, 128), F32),
             pltpu.VMEM((count, 128, 128), BF),
             pltpu.VMEM((128, 2048), BF),
             pltpu.VMEM((2048, 128), BF),
@@ -670,22 +709,24 @@
             pltpu.VMEM((x_length, 2048), F32),
             pltpu.VMEM((1024, 128), F32),
             pltpu.VMEM((1024, 128), F32),
-            pltpu.VMEM((count, 32, 128), BF),
-            pltpu.VMEM((count, 32, 128), BF),
-            pltpu.VMEM((count, 32, 128), BF),
-            pltpu.VMEM((count, 32, 128), BF),
+            pltpu.VMEM((count, 2, 16, 128), BF),
+            pltpu.VMEM((2, count, 16, 128), BF),
+            pltpu.VMEM((count, 2, 16, 128), BF),
+            pltpu.VMEM((2, count, 16, 128), BF),
             pltpu.VMEM((count, 1, 128), F32),
             pltpu.VMEM((count, 1, 128), F32),
             pltpu.VMEM((1, 128), F32),
+            pltpu.VMEM((count, 1, 128), F32),
+            dma((4,)),
             dma((near,)),
             dma((near,)),
             dma((2,)),
             dma((2, near)),
             dma((2, near)),
         ]
-        + [dma((count,))] * 8,
+        + [dma((2, count))] * 5,
         compiler_params=pltpu.CompilerParams(
-            collective_id=0, has_side_effects=True, vmem_limit_bytes=32 * 1024 * 1024
+            collective_id=0, has_side_effects=True, vmem_limit_bytes=60 * 1024 * 1024
         ),
         cost_estimate=pl.CostEstimate(
             flops=400_000_000, bytes_accessed=2_000_000, transcendentals=200_000
@@ -696,11 +737,9 @@
         lift_weight,
         spectral_weight,
         mix_weight,
-        project_weight,
+        jnp.transpose(project_weight),
         mode_index.reshape(1, -1),
     )
-    mix_grad = jnp.transpose(mix_rows.reshape(32, 2, 64), (1, 0, 2)).reshape(64, 64)
-    return (new_velocity, spectral_grad, mix_grad)
 
 
 def local(slot_field, solid, lift_weight, spectral_weight, mix_weight, project_weight, mode_index):

time: 44.8 us -> 43.3 us (0.967)
  local copies, waits for them, and re-layouts: 6.59 us -> 2.97 us
  Pallas kernels: 36.5 us -> 39.4 us
  other arithmetic: 0.68 us -> 0 us
    pallas_call x1, Pallas kernels: 36.5 us -> 39.4 us  [fused(): pl.pallas_call(functools.partial(fused_kernel, sizes), out_shape=(shape((...]
    unnamed x15 -> x7, local copies, waits for them, and re-layouts: 5.37 us -> 2.97 us
    pallas_call x1 -> x0, other arithmetic: 0.68 us -> none  [fused(): pl.pallas_call(functools.partial(fused_kernel, sizes), out_shape=(shape((...]
    transpose x1 -> x0, local copies, waits for them, and re-layouts: 0.62 us -> none  [fused(): jnp.transpose(mix_rows.reshape(32, 2, 64), (1, 0, 2)).reshape(64, 64)]
    pallas_call x1 -> x0, local copies, waits for them, and re-layouts: 0.51 us -> none  [fused(): pl.pallas_call(functools.partial(fused_kernel, sizes), out_shape=(shape((...]
where the time goes in v2:
time: 43.3 us; the launch traced here: 43 us
  Pallas kernels  39.4 us (91%)
  local copies, waits for them, and re-layouts  2.97 us (7%)
  between operations  0.65 us (2%)
    pallas_call x1, Pallas kernels, fused(): pl.pallas_call(functools.partial(fused_kernel, sizes), out_shape=(shape((...  39.4 us
    unnamed x7, local copies, waits for them, and re-layouts  2.97 us

profile of v2, /device:TPU:0, one launch (start us, length us, event | category | flops | bytes accessed | tf_op | source)
XLA Modules:
  0.0 43.0 jit_solution(11602158213902544698)
XLA Ops:
  0.6 39.4 %shard_map.94 = (f32[3,2,48,128]{3,2,1,0:T(8,128)}, f32[64,128]{1,0:T(8,128)}, f32[64,64]{1,0:T(8,128)}) custom-call(f32[1,2,48,128]{3,2,1,0:T(8,128)} %field_ref.1, s32[2,48,128]{2,1,0:T(8,128)} %solid_ref.1, bf16[3,64]{1,0:T(4,128)(2,1)} %lift_ref.1, bf16[2048,128]{1,0:T(8,128)(2,1)} %spec_ref.1, bf16[64,64]{1,0:T(8,128)(2,1)} %mix_ref.1, ...), custom_call_target="tpu_custom_call" | custom-call | flops 400000000 | bytes 2000000 | tf_op jit(solution)/shard_map/pallas_call | solution.py:688
  40.0 0.0 copy-start.1
  40.0 1.6 %copy.13 = f32[3,2,48,128]{3,2,1,0:T(8,128)} copy(f32[3,2,48,128]{3,2,1,0:T(8,128)} %get-tuple-element.6) | data formatting | bytes 294912
  41.6 0.0 copy-done.1
  41.6 0.0 copy-start
  41.6 0.6 %copy.14 = f32[64,128]{1,0:T(8,128)} copy(f32[64,128]{1,0:T(8,128)S(1)} %copy-done.1) | data formatting | bytes 65536
  42.2 0.2 copy-done
  42.4 0.6 %copy.15 = f32[64,64]{1,0:T(8,128)} copy(f32[64,64]{1,0:T(8,128)S(1)} %copy-done) | data formatting | bytes 32768
Async XLA Ops:
  40.0 1.6 %copy-start.1 = (f32[64,128]{1,0:T(8,128)S(1)}, f32[64,128]{1,0:T(8,128)}, u32[]{:S(2)}) copy-start(f32[64,128]{1,0:T(8,128)} %get-tuple-element.7) | copy-start | bytes 98308
  41.6 0.8 %copy-start = (f32[64,64]{1,0:T(8,128)S(1)}, f32[64,64]{1,0:T(8,128)}, u32[]{:S(2)}) copy-start(f32[64,64]{1,0:T(8,128)} %get-tuple-element.8) | copy-start | bytes 49156

commit v3 on v2

--- a/solution.py
+++ b/solution.py
@@ -225,6 +225,8 @@
     m_recv,
     m_row,
     m_all,
+    g_part,
+    g_recv,
     load,
     field_send,
     field_recv,
@@ -236,6 +238,7 @@
     d_sems_b,
     m_sems,
     r_sems,
+    g_sems,
 ):
     grps, gxs, gys, x_length, cell_total = sizes
     count = grps * gxs * gys
@@ -520,43 +523,49 @@
 
         lax.fori_loop(0, modes, step, 0, unroll=8)
 
-    def exchange(src, dst, sems, place, sent, landed):
+    def exchange(src, dst, sems, place, sent):
         return pltpu.make_async_remote_copy(
             src_ref=src,
             dst_ref=dst,
             send_sem=sems.at[0, sent],
-            recv_sem=sems.at[1, landed],
+            recv_sem=sems.at[1, 0],
             device_id=place,
             device_id_type=MESH,
         )
 
+    def keep_own(src, dst, sems):
+        pltpu.make_async_copy(src, dst, sems.at[1, 0]).start()
+
+    def await_all(buffer, sems):
+        pltpu.make_async_copy(buffer, buffer, sems.at[1, 0]).wait()
+
     def a_copy(place, t, at):
-        return exchange(a_own.at[t], a_all.at[at], a_sems, place, t, at)
+        return exchange(a_own.at[t], a_all.at[at], a_sems, place, t)
 
     def d_copy(part, place, t, at):
-        return exchange(d_own.at[part, t], d_all.at[part, at], d_sems[part], place, t, at)
+        return exchange(d_own.at[part, t], d_all.at[part, at], d_sems[part], place, t)
 
     def m_copy(place, t, at):
-        return exchange(m_part.at[t], m_recv.at[at], m_sems, place, t, at)
+        return exchange(m_part.at[t], m_recv.at[at], m_sems, place, t)
 
     def r_copy(place, t, at):
-        return exchange(m_row, m_all.at[at], r_sems, place, t, at)
+        return exchange(m_row, m_all.at[at], r_sems, place, t)
 
     def keep_a(m):
         def keep(rows):
             both = rows.astype(BF)
-            a_own[m, 0] = both[:16]
-            a_own[m, 1] = both[16:]
+            a_own[m // gys, m % gys, 0] = both[:16]
+            a_own[m // gys, m % gys, 1] = both[16:]
 
         mode_rows(m, pairs, keep)
 
     all_modes(keep_a)
-    for place, t in peers:
-        a_copy(place, t, me).start()
-    a_all[pl.ds(me, 1)] = a_own[pl.ds(me, 1)]
+    for place, t in near_peers:
+        a_copy(place, t, slot).start()
+    keep_own(a_own.at[slot], a_all.at[slot], a_sems)
 
     def mix_mode(m):
-        out = dot(a_own[m].reshape(lines, 2 * chans), wide_mix[m])
+        out = dot(a_own[m // gys, m % gys].reshape(lines, 2 * chans), wide_mix[m])
         top = jnp.concatenate([out[:8], out[16:24]], axis=0)
         bottom = jnp.concatenate([out[8:16], out[24:]], axis=0)
         stage_out[pl.ds(m, pairs, stride=64), :] = jnp.where(
@@ -617,47 +626,60 @@
                 m_part[row] = packed[row : row + 1, :]
             for place, t in peers:
                 m_copy(place, t, me).start()
-            m_recv[pl.ds(me, 1)] = m_part[pl.ds(me, 1)]
+            keep_own(m_part.at[me], m_recv.at[me], m_sems)
 
         def keep_d(m):
             def keep(rows):
-                d_own[half_lines, m] = rows.astype(BF)
+                d_own[half_lines, m // gys, m % gys] = rows.astype(BF)
 
             mode_rows(m, pairs // 2, keep)
 
         all_modes(keep_d)
-        for place, t in peers:
-            d_copy(half_lines, place, t, me).start()
-        d_all[half_lines, pl.ds(me, 1)] = d_own[half_lines, pl.ds(me, 1)]
-
-    for place, t in peers:
-        m_copy(place, t, t).wait_recv()
+        for place, t in near_peers:
+            d_copy(half_lines, place, t, slot).start()
+        keep_own(d_own.at[half_lines, slot], d_all.at[half_lines, slot], d_sems[half_lines])
+
+    await_all(m_recv, m_sems)
     total = jnp.sum(m_recv[...], axis=0)
     m_row[...] = total
-    m_all[pl.ds(me, 1)] = total[None]
+    keep_own(m_row, m_all.at[me], r_sems)
     for place, t in peers:
         r_copy(place, t, me).start()
 
-    for place, t in peers:
-        a_copy(place, t, t).wait_recv()
-    square_sum = jnp.zeros((128, 128), F32)
+    await_all(a_all, a_sems)
+    sums = [jnp.zeros((128, 128), F32) for _ in range(gys)]
     for half_lines in range(2):
-        for place, t in peers:
-            d_copy(half_lines, place, t, t).wait_recv()
-        a_lines = a_all[:, half_lines].reshape(count * 16, 2 * chans)
-        d_lines = d_all[half_lines].reshape(count * 16, 2 * chans)
-        square_sum = square_sum + dot(a_lines, d_lines, ((0,), (0,)))
-    turned_sum = pltpu.roll(square_sum[64:], 64, 1)
-    grad_ref[...] = square_sum[:64] + jnp.where(low_half, turned_sum, -turned_sum)
-
-    for place, t in peers:
-        r_copy(place, t, t).wait_recv()
+        await_all(d_all.at[half_lines], d_sems[half_lines])
+        for q in range(gys):
+            a_lines = a_all[:, q, half_lines].reshape(near * 16, 2 * chans)
+            d_lines = d_all[half_lines, :, q].reshape(near * 16, 2 * chans)
+            sums[q] = sums[q] + dot(a_lines, d_lines, ((0,), (0,)))
+    for q in range(gys):
+        turned_sum = pltpu.roll(sums[q][64:], 64, 1)
+        g_part[q] = sums[q][:64] + jnp.where(low_half, turned_sum, -turned_sum)
+
+    def g_copy(d):
+        place = {"grp": g, "gx": gx, "gy": y_at[d]}
+        return exchange(g_part.at[y_at[d]], g_recv.at[gy], g_sems, place, d)
+
+    for d in range(1, gys):
+        g_copy(d).start()
+    keep_own(g_part.at[gy], g_recv.at[gy], g_sems)
+    await_all(g_recv, g_sems)
+    grad_ref[...] = jnp.sum(g_recv[...], axis=0)
+
+    await_all(m_all, r_sems)
     rows = jnp.concatenate([m_all[row] for row in range(count)], axis=0)
     mixg_ref[...] = jnp.concatenate([rows[:, :64], rows[:, 64:]], axis=0)
 
     result_copy.wait()
     for place, s in near_peers:
         field_copy(place, s, slot).wait_send()
+        a_copy(place, s, slot).wait_send()
+        d_copy(0, place, s, slot).wait_send()
+        d_copy(1, place, s, slot).wait_send()
+    for d in range(1, gys):
+        g_copy(d).wait_send()
     solid_copy.wait_send()
 
     @pl.when(gy > 0)
@@ -669,9 +691,6 @@
         each_near(lambda s: rim_copy(1, s, slot).wait_send())
 
     for place, t in peers:
-        a_copy(place, t, me).wait_send()
-        d_copy(0, place, t, me).wait_send()
-        d_copy(1, place, t, me).wait_send()
         m_copy(place, t, me).wait_send()
         r_copy(place, t, me).wait_send()
 
@@ -709,14 +728,16 @@
             pltpu.VMEM((x_length, 2048), F32),
             pltpu.VMEM((1024, 128), F32),
             pltpu.VMEM((1024, 128), F32),
-            pltpu.VMEM((count, 2, 16, 128), BF),
-            pltpu.VMEM((2, count, 16, 128), BF),
-            pltpu.VMEM((count, 2, 16, 128), BF),
-            pltpu.VMEM((2, count, 16, 128), BF),
+            pltpu.VMEM((near, gys, 2, 16, 128), BF),
+            pltpu.VMEM((2, near, gys, 16, 128), BF),
+            pltpu.VMEM((near, gys, 2, 16, 128), BF),
+            pltpu.VMEM((2, near, gys, 16, 128), BF),
             pltpu.VMEM((count, 1, 128), F32),
             pltpu.VMEM((count, 1, 128), F32),
             pltpu.VMEM((1, 128), F32),
             pltpu.VMEM((count, 1, 128), F32),
+            pltpu.VMEM((gys, 64, 128), F32),
+            pltpu.VMEM((gys, 64, 128), F32),
             dma((4,)),
             dma((near,)),
             dma((near,)),
@@ -724,7 +745,7 @@
             dma((2, near)),
             dma((2, near)),
         ]
-        + [dma((2, count))] * 5,
+        + [dma((2, count))] * 6,
         compiler_params=pltpu.CompilerParams(
             collective_id=0, has_side_effects=True, vmem_limit_bytes=60 * 1024 * 1024
         ),

time: 43.3 us -> 40.4 us (0.933)
  Pallas kernels: 39.4 us -> 36.5 us
    pallas_call x1, Pallas kernels: 39.4 us -> 36.5 us  [fused(): pl.pallas_call(functools.partial(fused_kernel, sizes), out_shape=(shape((...]
where the time goes in v3:
time: 40.4 us; the launch traced here: 40.1 us
  Pallas kernels  36.5 us (90%)
  local copies, waits for them, and re-layouts  2.97 us (7%)
  between operations  0.65 us (2%)
    pallas_call x1, Pallas kernels, fused(): pl.pallas_call(functools.partial(fused_kernel, sizes), out_shape=(shape((...  36.5 us
    unnamed x7, local copies, waits for them, and re-layouts  2.97 us

profile of v3, /device:TPU:0, one launch (start us, length us, event | category | flops | bytes accessed | tf_op | source)
XLA Modules:
  0.0 40.1 jit_solution(14926125238518864742)
XLA Ops:
  0.6 36.5 %shard_map.94 = (f32[3,2,48,128]{3,2,1,0:T(8,128)}, f32[64,128]{1,0:T(8,128)}, f32[64,64]{1,0:T(8,128)}) custom-call(f32[1,2,48,128]{3,2,1,0:T(8,128)} %field_ref.1, s32[2,48,128]{2,1,0:T(8,128)} %solid_ref.1, bf16[3,64]{1,0:T(4,128)(2,1)} %lift_ref.1, bf16[2048,128]{1,0:T(8,128)(2,1)} %spec_ref.1, bf16[64,64]{1,0:T(8,128)(2,1)} %mix_ref.1, ...), custom_call_target="tpu_custom_call" | custom-call | flops 400000000 | bytes 2000000 | tf_op jit(solution)/shard_map/pallas_call | solution.py:707
  37.1 0.0 copy-start.1
  37.1 1.6 %copy.13 = f32[3,2,48,128]{3,2,1,0:T(8,128)} copy(f32[3,2,48,128]{3,2,1,0:T(8,128)} %get-tuple-element.6) | data formatting | bytes 294912
  38.7 0.0 copy-done.1
  38.7 0.0 copy-start
  38.7 0.6 %copy.14 = f32[64,128]{1,0:T(8,128)} copy(f32[64,128]{1,0:T(8,128)S(1)} %copy-done.1) | data formatting | bytes 65536
  39.3 0.2 copy-done
  39.5 0.6 %copy.15 = f32[64,64]{1,0:T(8,128)} copy(f32[64,64]{1,0:T(8,128)S(1)} %copy-done) | data formatting | bytes 32768
Async XLA Ops:
  37.1 1.6 %copy-start.1 = (f32[64,128]{1,0:T(8,128)S(1)}, f32[64,128]{1,0:T(8,128)}, u32[]{:S(2)}) copy-start(f32[64,128]{1,0:T(8,128)} %get-tuple-element.7) | copy-start | bytes 98308
  38.7 0.8 %copy-start = (f32[64,64]{1,0:T(8,128)S(1)}, f32[64,64]{1,0:T(8,128)}, u32[]{:S(2)}) copy-start(f32[64,64]{1,0:T(8,128)} %get-tuple-element.8) | copy-start | bytes 49156

commit v4 on v3

--- a/solution.py
+++ b/solution.py
@@ -225,6 +225,8 @@
     m_recv,
     m_row,
     m_all,
+    m_plane,
+    m_planes,
     g_part,
     g_recv,
     load,
@@ -239,6 +241,7 @@
     m_sems,
     r_sems,
     g_sems,
+    z_sems,
 ):
     grps, gxs, gys, x_length, cell_total = sizes
     count = grps * gxs * gys
@@ -623,10 +626,10 @@
                 iota((32, 128), 1) < 64, mix_own[:32], pltpu.roll(mix_own[32:], 64, 1)
             )
             for row in range(count):
-                m_part[row] = packed[row : row + 1, :]
-            for place, t in peers:
-                m_copy(place, t, me).start()
-            keep_own(m_part.at[me], m_recv.at[me], m_sems)
+                m_part[row // gys, row % gys] = packed[row : row + 1, :]
+            for place, t in near_peers:
+                m_copy(place, t, slot).start()
+            keep_own(m_part.at[slot], m_recv.at[slot], m_sems)
 
         def keep_d(m):
             def keep(rows):
@@ -640,11 +643,15 @@
         keep_own(d_own.at[half_lines, slot], d_all.at[half_lines, slot], d_sems[half_lines])
 
     await_all(m_recv, m_sems)
-    total = jnp.sum(m_recv[...], axis=0)
-    m_row[...] = total
-    keep_own(m_row, m_all.at[me], r_sems)
-    for place, t in peers:
-        r_copy(place, t, me).start()
+    m_plane[...] = jnp.sum(m_recv[...], axis=0)
+
+    def mz_copy(d):
+        place = {"grp": g, "gx": gx, "gy": y_at[d]}
+        return exchange(m_plane, m_planes.at[gy], z_sems, place, d)
+
+    for d in range(1, gys):
+        mz_copy(d).start()
+    keep_own(m_plane, m_planes.at[gy], z_sems)
 
     await_all(a_all, a_sems)
     sums = [jnp.zeros((128, 128), F32) for _ in range(gys)]
@@ -665,11 +672,16 @@
     for d in range(1, gys):
         g_copy(d).start()
     keep_own(g_part.at[gy], g_recv.at[gy], g_sems)
+    await_all(m_planes, z_sems)
+    m_row[...] = jnp.sum(m_planes[...], axis=0)
+    for place, t in near_peers:
+        r_copy(place, t, slot).start()
+    keep_own(m_row, m_all.at[slot], r_sems)
     await_all(g_recv, g_sems)
     grad_ref[...] = jnp.sum(g_recv[...], axis=0)
 
     await_all(m_all, r_sems)
-    rows = jnp.concatenate([m_all[row] for row in range(count)], axis=0)
+    rows = jnp.concatenate([m_all[row // gys, row % gys] for row in range(count)], axis=0)
     mixg_ref[...] = jnp.concatenate([rows[:, :64], rows[:, 64:]], axis=0)
 
     result_copy.wait()
@@ -678,8 +690,11 @@
         a_copy(place, s, slot).wait_send()
         d_copy(0, place, s, slot).wait_send()
         d_copy(1, place, s, slot).wait_send()
+        m_copy(place, s, slot).wait_send()
+        r_copy(place, s, slot).wait_send()
     for d in range(1, gys):
         g_copy(d).wait_send()
+        mz_copy(d).wait_send()
     solid_copy.wait_send()
 
     @pl.when(gy > 0)
@@ -689,10 +704,6 @@
     @pl.when(gy < gys - 1)
     def _():
         each_near(lambda s: rim_copy(1, s, slot).wait_send())
-
-    for place, t in peers:
-        m_copy(place, t, me).wait_send()
-        r_copy(place, t, me).wait_send()
 
 
 def fused(sizes, slot_field, solid, lift_weight, spectral_weight, mix_weight, project_weight, mode_index):
@@ -732,10 +743,12 @@
             pltpu.VMEM((2, near, gys, 16, 128), BF),
             pltpu.VMEM((near, gys, 2, 16, 128), BF),
             pltpu.VMEM((2, near, gys, 16, 128), BF),
-            pltpu.VMEM((count, 1, 128), F32),
-            pltpu.VMEM((count, 1, 128), F32),
-            pltpu.VMEM((1, 128), F32),
-            pltpu.VMEM((count, 1, 128), F32),
+            pltpu.VMEM((near, gys, 1, 128), F32),
+            pltpu.VMEM((near, gys, 1, 128), F32),
+            pltpu.VMEM((gys, 1, 128), F32),
+            pltpu.VMEM((near, gys, 1, 128), F32),
+            pltpu.VMEM((gys, 1, 128), F32),
+            pltpu.VMEM((gys, gys, 1, 128), F32),
             pltpu.VMEM((gys, 64, 128), F32),
             pltpu.VMEM((gys, 64, 128), F32),
             dma((4,)),
@@ -745,7 +758,7 @@
             dma((2, near)),
             dma((2, near)),
         ]
-        + [dma((2, count))] * 6,
+        + [dma((2, count))] * 7,
         compiler_params=pltpu.CompilerParams(
             collective_id=0, has_side_effects=True, vmem_limit_bytes=60 * 1024 * 1024
         ),

time: 40.4 us -> 40.1 us (level)
  no operation moved by 1% of the time
where the time goes in v4:
time: 40.1 us; the launch traced here: 39.8 us
  Pallas kernels  36.2 us (90%)
  local copies, waits for them, and re-layouts  2.97 us (7%)
  between operations  0.65 us (2%)
    pallas_call x1, Pallas kernels, fused(): pl.pallas_call(functools.partial(fused_kernel, sizes), out_shape=(shape((...  36.2 us
    unnamed x7, local copies, waits for them, and re-layouts  2.97 us

profile of v4, /device:TPU:0, one launch (start us, length us, event | category | flops | bytes accessed | tf_op | source)
XLA Modules:
  0.0 39.8 jit_solution(14496768148697606951)
XLA Ops:
  0.6 36.2 %shard_map.94 = (f32[3,2,48,128]{3,2,1,0:T(8,128)}, f32[64,128]{1,0:T(8,128)}, f32[64,64]{1,0:T(8,128)}) custom-call(f32[1,2,48,128]{3,2,1,0:T(8,128)} %field_ref.1, s32[2,48,128]{2,1,0:T(8,128)} %solid_ref.1, bf16[3,64]{1,0:T(4,128)(2,1)} %lift_ref.1, bf16[2048,128]{1,0:T(8,128)(2,1)} %spec_ref.1, bf16[64,64]{1,0:T(8,128)(2,1)} %mix_ref.1, ...), custom_call_target="tpu_custom_call" | custom-call | flops 400000000 | bytes 2000000 | tf_op jit(solution)/shard_map/pallas_call | solution.py:718
  36.8 0.0 copy-start.1
  36.8 1.6 %copy.13 = f32[3,2,48,128]{3,2,1,0:T(8,128)} copy(f32[3,2,48,128]{3,2,1,0:T(8,128)} %get-tuple-element.6) | data formatting | bytes 294912
  38.4 0.0 copy-done.1
  38.4 0.0 copy-start
  38.4 0.6 %copy.14 = f32[64,128]{1,0:T(8,128)} copy(f32[64,128]{1,0:T(8,128)S(1)} %copy-done.1) | data formatting | bytes 65536
  39.0 0.2 copy-done
  39.2 0.6 %copy.15 = f32[64,64]{1,0:T(8,128)} copy(f32[64,64]{1,0:T(8,128)S(1)} %copy-done) | data formatting | bytes 32768
Async XLA Ops:
  36.8 1.6 %copy-start.1 = (f32[64,128]{1,0:T(8,128)S(1)}, f32[64,128]{1,0:T(8,128)}, u32[]{:S(2)}) copy-start(f32[64,128]{1,0:T(8,128)} %get-tuple-element.7) | copy-start | bytes 98308
  38.4 0.8 %copy-start = (f32[64,64]{1,0:T(8,128)S(1)}, f32[64,64]{1,0:T(8,128)}, u32[]{:S(2)}) copy-start(f32[64,64]{1,0:T(8,128)} %get-tuple-element.8) | copy-start | bytes 49156
